TPU v7x, 256 devices: a whole 4x4x8 slice. The times are simulated.
256 devices in a mesh: tile: 64 (over z_hi, x, y, core), head: 4 (over z_lo).
Axes of the slice: x: 4, y: 4, z: 8 (z_hi: 2, z_lo: 4; z = z_hi * 4 + z_lo), core: 2. Of those that a mesh axis runs over, the one named last changes fastest.
Arguments:
- queries: bfloat16 [65536, 1024], P('tile', 'head'), may hold values from -240 to 240
- keys: bfloat16 [65536, 1024], P('tile', 'head'), may hold values from -6 to 6, as said below
- values: bfloat16 [65536, 1024], P('tile', 'head'), may hold values from -6 to 6
- out_weight: bfloat16 [1024, 1024], replicated, may hold values from -0.1875 to 0.1875
- cotangent: bfloat16 [65536, 1024], P('tile', 'head'), may hold values from -6 to 6
Outputs:
- output: bfloat16 [65536, 1024], P('tile', 'head')
- grad_queries: bfloat16 [65536, 1024], P('tile', 'head')
- grad_keys: bfloat16 [65536, 1024], P('tile', 'head')
- grad_values: bfloat16 [65536, 1024], P('tile', 'head')
- weight_grad: float32 [1024, 1024], P('head')
Inputs may be any that keep to these rules, and one draw needn't show every extreme that they name: keys of order one.
All inputs are finite; a program needn't handle non-finite values.
Results may differ from a plain program's by a relative error of at most 0.015.
Values may be sent and summed in bfloat16 or wider, within the bound.
A program may use at most 192 MiB of HBM per device.

v0:
```python
import math

import jax
import jax.numpy as jnp
from jax import lax
from jax.sharding import PartitionSpec as P

D = 1024
HEADS = 16
TILE = 256
POOLED = 64


ROOT_HALF = 1.0 / math.sqrt(2.0)


def swapped(block, axis, stride):
    count = lax.axis_size(axis)
    route = []
    for low in range(count):
        high = low | 1 << stride
        if high != low and high < count:
            route += [(low, high), (high, low)]
    return lax.ppermute(block, axis, route)


def pool_nodes(nodes):
    count = nodes.shape[0]
    summed = nodes.astype(jnp.float32).reshape(count // 2, POOLED, 2, nodes.shape[2]).sum(2)
    return (summed * ROOT_HALF).astype(jnp.bfloat16)


def flip_pairs(nodes):
    count = nodes.shape[0]
    return nodes.reshape(count // 2, 2, POOLED, nodes.shape[2])[:, ::-1].reshape(
        count, POOLED, nodes.shape[2]
    )


def spread_nodes(nodes):
    count = nodes.shape[0]
    return jnp.repeat(nodes * ROOT_HALF, 2, axis=1).reshape(2 * count, POOLED, nodes.shape[2])


def join_pair(own_node, other_node, upper):
    left_node = jnp.where(upper, other_node, own_node)
    right_node = jnp.where(upper, own_node, other_node)
    return pool_nodes(jnp.stack([left_node, right_node]))[0]


def local(queries, keys, values, out_weight, cotangent):
    rows, width = queries.shape
    per_head = D // HEADS
    heads_here = width // per_head
    tiles = rows // TILE
    group = TILE // POOLED
    local_levels = tiles.bit_length() - 1
    tile_count = lax.axis_size("tile")
    device_levels = tile_count.bit_length() - 1
    position = lax.axis_index("tile")
    head_position = lax.axis_index("head")
    scale = 1.0 / math.sqrt(per_head)

    def summarize(tokens):
        total = tokens.astype(jnp.float32).reshape(tiles * POOLED, group, width).sum(1)
        return (total * (1.0 / math.sqrt(group))).astype(jnp.bfloat16).reshape(tiles, POOLED, width)

    node_k = summarize(keys)
    node_v = summarize(values)
    far_k = []
    far_v = []
    for level_no in range(local_levels):
        far_k.append(jnp.repeat(flip_pairs(node_k), 2**level_no, axis=0))
        far_v.append(jnp.repeat(flip_pairs(node_v), 2**level_no, axis=0))
        node_k = pool_nodes(node_k)
        node_v = pool_nodes(node_v)
    top_k = node_k[0]
    top_v = node_v[0]
    upper_k = []
    upper_v = []
    own_k, own_v = (top_k, top_v)
    for bit_no in range(device_levels):
        other_k, other_v = swapped((own_k, own_v), "tile", bit_no)
        upper_k.append(other_k)
        upper_v.append(other_v)
        if bit_no + 1 < device_levels:
            upper = position >> bit_no & 1 == 1
            own_k = join_pair(own_k, other_k, upper)
            own_v = join_pair(own_v, other_v, upper)
    far_k = far_k + [jnp.broadcast_to(entry[None], (tiles, POOLED, width)) for entry in upper_k]
    far_v = far_v + [jnp.broadcast_to(entry[None], (tiles, POOLED, width)) for entry in upper_v]
    key_all = jnp.concatenate([keys.reshape(tiles, TILE, width)] + far_k, axis=1).reshape(
        tiles, -1, heads_here, per_head
    )
    value_all = jnp.concatenate([values.reshape(tiles, TILE, width)] + far_v, axis=1).reshape(
        tiles, -1, heads_here, per_head
    )
    query_blocks = queries.reshape(tiles, TILE, heads_here, per_head)
    scores = (
        jnp.einsum("tqhd,tkhd->thqk", query_blocks, key_all, preferred_element_type=jnp.float32)
        * scale
    )
    top_score = jnp.max(scores, axis=-1, keepdims=True)
    weights = jnp.exp(scores - top_score)
    probs = weights / jnp.sum(weights, axis=-1, keepdims=True)
    probs_low = probs.astype(jnp.bfloat16)
    mixed = jnp.einsum("thqk,tkhd->tqhd", probs_low, value_all, preferred_element_type=jnp.float32)
    mixed = mixed.astype(jnp.bfloat16).reshape(rows, width)
    own_rows = lax.dynamic_slice_in_dim(out_weight, head_position * width, width, 0)
    terms = jnp.dot(mixed, own_rows, preferred_element_type=jnp.float32)
    output = lax.psum_scatter(terms.astype(jnp.bfloat16), "head", scatter_dimension=1, tiled=True)
    upstream = lax.all_gather(cotangent, "head", axis=1, tiled=True)
    grad_mixed = lax.dot_general(
        upstream, own_rows, (((1,), (1,)), ((), ())), preferred_element_type=jnp.float32
    ).astype(jnp.bfloat16)
    weight_part = lax.dot_general(
        mixed, upstream, (((0,), (0,)), ((), ())), preferred_element_type=jnp.float32
    )
    weight_grad = lax.psum(weight_part, "tile")
    grad_blocks = grad_mixed.reshape(tiles, TILE, heads_here, per_head)
    grad_probs = jnp.einsum(
        "tqhd,tkhd->thqk", grad_blocks, value_all, preferred_element_type=jnp.float32
    )
    centre = jnp.sum(probs * grad_probs, axis=-1, keepdims=True)
    dscore = (probs * (grad_probs - centre) * scale).astype(jnp.bfloat16)
    grad_queries = jnp.einsum(
        "thqk,tkhd->tqhd", dscore, key_all, preferred_element_type=jnp.float32
    )
    grad_queries = grad_queries.astype(jnp.bfloat16).reshape(rows, width)
    grad_key = jnp.einsum(
        "thqk,tqhd->tkhd", dscore, query_blocks, preferred_element_type=jnp.float32
    ).reshape(tiles, -1, width)
    grad_value = jnp.einsum(
        "thqk,tqhd->tkhd", probs_low, grad_blocks, preferred_element_type=jnp.float32
    ).reshape(tiles, -1, width)
    levels = local_levels + device_levels
    far_key = grad_key[:, TILE:].reshape(tiles, levels, POOLED, width)
    far_value = grad_value[:, TILE:].reshape(tiles, levels, POOLED, width)
    carry_k = jnp.zeros((POOLED, width), jnp.float32)
    carry_v = jnp.zeros((POOLED, width), jnp.float32)
    for bit_no in reversed(range(device_levels)):
        level_k = far_key[:, local_levels + bit_no].sum(0)
        level_v = far_value[:, local_levels + bit_no].sum(0)
        if bit_no + 1 < device_levels:
            upper = position >> bit_no & 1 == 1
            spread_k = jnp.repeat(carry_k * ROOT_HALF, 2, axis=0)
            spread_v = jnp.repeat(carry_v * ROOT_HALF, 2, axis=0)
            kept_k = jnp.where(upper, spread_k[POOLED:], spread_k[:POOLED])
            kept_v = jnp.where(upper, spread_v[POOLED:], spread_v[:POOLED])
            level_k = level_k + jnp.where(upper, spread_k[:POOLED], spread_k[POOLED:])
            level_v = level_v + jnp.where(upper, spread_v[:POOLED], spread_v[POOLED:])
        else:
            kept_k = jnp.zeros((POOLED, width), jnp.float32)
            kept_v = jnp.zeros((POOLED, width), jnp.float32)
        taken_k, taken_v = (
            swapped(level_k.astype(jnp.bfloat16), "tile", bit_no).astype(level_k.dtype),
            swapped(level_v.astype(jnp.bfloat16), "tile", bit_no).astype(level_v.dtype),
        )
        carry_k = kept_k + taken_k
        carry_v = kept_v + taken_v
    down_k = carry_k[None]
    down_v = carry_v[None]
    for level_no in reversed(range(local_levels)):
        part_k = flip_pairs(
            far_key[:, level_no].reshape(tiles >> level_no, 2**level_no, POOLED, width).sum(1)
        )
        part_v = flip_pairs(
            far_value[:, level_no].reshape(tiles >> level_no, 2**level_no, POOLED, width).sum(1)
        )
        down_k = part_k + spread_nodes(down_k)
        down_v = part_v + spread_nodes(down_v)
    factor = 1.0 / math.sqrt(group)
    back_k = jnp.repeat(down_k.reshape(tiles * POOLED, width) * factor, group, axis=0)
    back_v = jnp.repeat(down_v.reshape(tiles * POOLED, width) * factor, group, axis=0)
    grad_keys = (grad_key[:, :TILE].reshape(rows, width) + back_k).astype(jnp.bfloat16)
    grad_values = (grad_value[:, :TILE].reshape(rows, width) + back_v).astype(jnp.bfloat16)
    return (output, grad_queries, grad_keys, grad_values, weight_grad)


def solution(mesh):
    in_specs = (P("tile", "head"), P("tile", "head"), P("tile", "head"), P(), P("tile", "head"))
    out_specs = (
        P("tile", "head"),
        P("tile", "head"),
        P("tile", "head"),
        P("tile", "head"),
        P("head", None),
    )
    return jax.shard_map(local, mesh=mesh, in_specs=in_specs, out_specs=out_specs, check_vma=False)
```

profile of v0, /device:TPU:1, one launch (start us, length us, event | category | flops | bytes accessed | tf_op | source)
XLA Modules:
  0.0 966.6 jit_solution(12694286872101046332)
XLA Ops:
  7.2 1.4 reshape.554
  10.7 3.2 collective-permute-start
  13.9 1.3 reshape.563
  15.2 1.4 reduce_sum.304
  21.1 1.5 collective-permute-start.7
  26.0 1.9 collective-permute-start.8
  28.7 1.8 collective-permute-done.8
  32.9 2.5 collective-permute-start.4
  36.3 1.5 collective-permute-start.10
  38.7 7.5 collective-permute-start.5
  47.2 1.9 collective-permute-start.11
  49.0 2.8 reshape.571
  52.5 2.0 reshape.572
  55.1 2.2 copy.37
  62.2 2.0 reshape.574
  66.3 1.5 copy.81
  68.7 1.5 copy.82
  71.1 1.5 copy.83
  72.5 1.5 copy.76
  74.0 1.5 copy.84
  75.5 1.5 copy.77
  77.0 1.5 copy.85
  78.5 1.5 copy.78
  82.6 1.6 broadcast_in_dim.191
  84.2 3.9 concatenate.23
  88.1 1.5 copy.86
  94.8 1.6 broadcast_in_dim.204
  96.4 3.8 concatenate.27
  100.2 10.3 %fusion.52 = (f32[4,4,256]{2,1,0:T(4,128)S(1)}, f32[4,4,256,768]{2,3,1,0:T(8,128)}) fusion(bf16[4,768,4,64]{1,3,2,0:T(8,128)(2,1)} %concatenate.27, bf16[4,256,4,64]{1,3,2,0:T(8,128)(2,1)} %copy.49), kind=kOutput, calls=%fused_computation.150 | convolution fusion | flops 412091136 | bytes 14696448 | tf_op jit(solution)/shard_map/sub | solution.py:104
  110.4 6.3 fusion.27
  117.3 3.3 fusion.53
  120.8 2.2 convolution_convert_fusion
  123.0 2.3 fusion.30
  125.8 7.8 fusion.37
  133.6 20.2 %fusion.31 = bf16[4,256,4,64]{1,3,2,0:T(8,128)(2,1)} fusion(bf16[4,768,4,64]{1,3,2,0:T(8,128)(2,1)S(1)} %copy-done.3, f32[4,4,256,768]{2,3,1,0:T(8,128)} %fusion.37, f32[4,4,256,768]{2,3,1,0:T(8,128)} %get-tuple-element.67, f32[4,4,256]{2,1,0:T(4,128)S(1)} %get-tuple-element.66), kind=kOutput, calls=%fused_computation.24 | convolution fusion | flops 424940288 | bytes 27279360 | tf_op jit(solution)/shard_map/thqk,tkhd->tqhd/dot_general | solution.py:126
  153.8 19.2 %fusion.12 = f32[4,4,768,64]{2,3,1,0:T(8,128)} fusion(bf16[4,256,4,64]{1,3,2,0:T(8,128)(2,1)S(1)} %copy-done.5, f32[4,4,256,768]{2,3,1,0:T(8,128)} %fusion.37, f32[4,4,256,768]{2,3,1,0:T(8,128)} %get-tuple-element.67, f32[4,4,256]{2,1,0:T(4,128)S(1)} %get-tuple-element.66), kind=kOutput, calls=%fused_computation.12 | convolution fusion | flops 424678144 | bytes 28852224 | tf_op jit(solution)/shard_map/thqk,tqhd->tkhd/dot_general | solution.py:130
  173.0 3.1 slice.221
  176.2 2.3 slice.220
  178.5 6.6 fusion.17
  186.4 1.5 copy.87
  188.0 1.5 reshape.573
  189.4 3.0 copy.91
  192.5 2.4 slice_reduce_fusion.6
  194.9 3.5 collective-permute-start.12
  199.1 2.5 copy.59
  201.7 1.9 copy.92
  203.5 2.3 slice_reduce_fusion
  205.9 2.1 collective-permute-start.18
  208.8 1.3 copy.63
  211.8 1.5 collective-permute-start.13
  213.6 1.7 collective-permute-start.19
  215.3 1.3 collective-permute-done.13
  219.5 1.3 collective-permute-done.14
  223.1 3.0 collective-permute-start.21
  231.3 8.6 collective-permute-start.17
  240.1 1.5 add_convert_fusion
  242.3 1.5 collective-permute-start.23
  246.4 1.3 reshape.545
  249.3 1.4 reshape.552
  250.6 2.4 fusion.35
  253.1 2.4 fusion.34
  255.5 649.0 %all-reduce.2.cloned.1.call-done = f32[256,1024]{1,0:T(8,128)} async-done(((f32[256,1024]{1,0:T(8,128)}), f32[256,1024]{1,0:T(8,128)}) %all-reduce.2.cloned.1.call-update) | async-done | bytes 1048592 | tf_op jit(solution)/shard_map/psum | solution.py:119
  904.5 52.8 %reduce-scatter.2.cloned.1.call-done = bf16[1024,256]{1,0:T(8,128)(2,1)} async-done(((bf16[1024,1024]{1,0:T(8,128)(2,1)}), bf16[1024,256]{1,0:T(8,128)(2,1)}) %reduce-scatter.2.cloned.1.call-update) | async-done | bytes 524304 | tf_op jit(solution)/shard_map/reduce_scatter | solution.py:111
  957.3 2.3 copy.99
  (251 shorter events, 54.0 us)
Async XLA Ops:
  7.2 113.7 %copy-start = (bf16[1024,1024]{1,0:T(8,128)(2,1)S(1)}, bf16[1024,1024]{1,0:T(8,128)(2,1)}, u32[]{:S(2)}) copy-start(bf16[1024,1024]{1,0:T(8,128)(2,1)} %param.8) | copy-start | bytes 6291460
  7.2 110.1 %all-gather.2.cloned.1.call-start = ((), (), s32[]{:S(2)}) async-start(), calls=%async_computation.2 | async-start | bytes 2621440 | tf_op jit(solution)/shard_map/all_gather | solution.py:112
  10.0 5.2 copy-start.4
  10.7 7.8 collective-permute-start
  18.3 1.3 collective-permute-start.6
  18.4 886.1 %all-reduce.2.cloned.1.call-start = ((), (), s32[]{:S(2)}) async-start(), calls=%async_computation.3 | async-start | bytes 2097152 | tf_op jit(solution)/shard_map/psum | solution.py:119
  19.6 0.9 copy-start.6
  20.7 2.9 collective-permute-start.1
  21.1 4.0 collective-permute-start.7
  23.6 28.2 %copy-start.7 = (bf16[64,256]{1,0:T(8,128)(2,1)}, bf16[64,256]{1,0:T(8,128)(2,1)S(1)}, u32[]{:S(2)}) copy-start(bf16[64,256]{1,0:T(8,128)(2,1)S(1)} %collective-permute-done.1) | copy-start | bytes 98308
  23.9 4.4 collective-permute-start.2
  25.2 0.6 copy-start.8
  26.0 4.5 collective-permute-start.8
  28.2 23.6 %copy-start.9 = (bf16[64,256]{1,0:T(8,128)(2,1)}, bf16[64,256]{1,0:T(8,128)(2,1)S(1)}, u32[]{:S(2)}) copy-start(bf16[64,256]{1,0:T(8,128)(2,1)S(1)} %collective-permute-done.2) | copy-start | bytes 98308
  28.5 4.0 collective-permute-start.3
  30.5 0.6 copy-start.10
  31.4 4.0 collective-permute-start.9
  32.6 19.2 %copy-start.11 = (bf16[64,256]{1,0:T(8,128)(2,1)}, bf16[64,256]{1,0:T(8,128)(2,1)S(1)}, u32[]{:S(2)}) copy-start(bf16[64,256]{1,0:T(8,128)(2,1)S(1)} %collective-permute-done.3) | copy-start | bytes 98308
  32.9 5.0 collective-permute-start.4
  35.4 0.6 copy-start.12
  36.3 10.0 %collective-permute-start.10 = (bf16[64,256]{1,0:T(8,128)(2,1)S(1)}, bf16[64,256]{1,0:T(8,128)(2,1)S(1)}, u32[]{:S(2)}, u32[]{:S(2)}) collective-permute-start(bf16[64,256]{1,0:T(8,128)(2,1)S(1)} %multiply_convert_fusion.6), channel_id=1, source_target_pairs={{0,64},{64,0},{4,68},{68,4},{8,72},{72,8},{12,76},{76,12},{16,80},... | collective-permute-start | bytes 98312 | tf_op jit(solution)/shard_map/ppermute | solution.py:24
  37.9 14.0 %copy-start.13 = (bf16[64,256]{1,0:T(8,128)(2,1)}, bf16[64,256]{1,0:T(8,128)(2,1)S(1)}, u32[]{:S(2)}) copy-start(bf16[64,256]{1,0:T(8,128)(2,1)S(1)} %collective-permute-done.4) | copy-start | bytes 98308
  38.7 39.7 %collective-permute-start.5 = (bf16[64,256]{1,0:T(8,128)(2,1)}, bf16[64,256]{1,0:T(8,128)(2,1)}, u32[]{:S(2)}, u32[]{:S(2)}) collective-permute-start(bf16[64,256]{1,0:T(8,128)(2,1)} %multiply_convert_fusion.11), channel_id=1, source_target_pairs={{0,128},{128,0},{4,132},{132,4},{8,136},{136,8},{12,140},{140,12},... | collective-permute-start | bytes 98312 | tf_op jit(solution)/shard_map/ppermute | solution.py:24
  46.3 5.5 copy-start.14
  47.2 40.9 %collective-permute-start.11 = (bf16[64,256]{1,0:T(8,128)(2,1)}, bf16[64,256]{1,0:T(8,128)(2,1)}, u32[]{:S(2)}, u32[]{:S(2)}) collective-permute-start(bf16[64,256]{1,0:T(8,128)(2,1)} %multiply_convert_fusion.5), channel_id=1, source_target_pairs={{0,128},{128,0},{4,132},{132,4},{8,136},{136,8},{12,140},{140,12},... | collective-permute-start | bytes 98312 | tf_op jit(solution)/shard_map/ppermute | solution.py:24
  120.6 836.7 %reduce-scatter.2.cloned.1.call-start = ((), (), s32[]{:S(2)}) async-start(), calls=%async_computation.1 | async-start | bytes 2621440 | tf_op jit(solution)/shard_map/reduce_scatter | solution.py:111
  125.4 8.2 copy-start.3
  133.6 20.2 %copy-start.5 = (bf16[4,256,4,64]{1,3,2,0:T(8,128)(2,1)S(1)}, bf16[4,256,4,64]{1,3,2,0:T(8,128)(2,1)}, u32[]{:S(2)}) copy-start(bf16[4,256,4,64]{1,3,2,0:T(8,128)(2,1)} %copy.49) | copy-start | bytes 1572868
  189.4 19.3 %copy-start.2 = (f32[4,256,256]{1,2,0:T(8,128)S(1)}, f32[4,256,256]{1,2,0:T(8,128)}, u32[]{:S(2)}) copy-start(f32[4,256,256]{1,2,0:T(8,128)} %slice.240) | copy-start | bytes 3145732
  194.9 15.2 %collective-permute-start.12 = (bf16[64,256]{1,0:T(8,128)(2,1)}, bf16[64,256]{1,0:T(8,128)(2,1)}, u32[]{:S(2)}, u32[]{:S(2)}) collective-permute-start(bf16[64,256]{1,0:T(8,128)(2,1)} %get-tuple-element.21), channel_id=1, source_target_pairs={{0,128},{128,0},{4,132},{132,4},{8,136},{136,8},{12,140},{140,12},... | collective-permute-start | bytes 98312 | tf_op jit(solution)/shard_map/ppermute | solution.py:24
  205.9 7.4 collective-permute-start.18
  211.8 4.8 collective-permute-start.13
  213.6 4.8 collective-permute-start.19
  217.6 3.3 collective-permute-start.14
  218.6 741.0 %copy-start.1 = (bf16[1024,1024]{1,0:T(8,128)(2,1)S(1)}, bf16[1024,1024]{1,0:T(8,128)(2,1)}, u32[]{:S(2)}) copy-start(bf16[1024,1024]{1,0:T(8,128)(2,1)} %param.8) | copy-start | bytes 6291460
  218.7 3.3 collective-permute-start.20
  221.8 4.4 collective-permute-start.15
  223.1 4.4 collective-permute-start.21
  227.1 3.3 collective-permute-start.16
  228.6 11.3 %collective-permute-start.22 = (bf16[64,256]{1,0:T(8,128)(2,1)S(1)}, bf16[64,256]{1,0:T(8,128)(2,1)S(1)}, u32[]{:S(2)}, u32[]{:S(2)}) collective-permute-start(bf16[64,256]{1,0:T(8,128)(2,1)S(1)} %add_convert_fusion.1), channel_id=1, source_target_pairs={{0,8},{8,0},{4,12},{12,4},{16,24},{24,16},{20,28},{28,20},{32,40},... | collective-permute-start | bytes 98312 | tf_op jit(solution)/shard_map/ppermute | solution.py:24
  231.3 12.5 %collective-permute-start.17 = (bf16[64,256]{1,0:T(8,128)(2,1)S(1)}, bf16[64,256]{1,0:T(8,128)(2,1)S(1)}, u32[]{:S(2)}, u32[]{:S(2)}) collective-permute-start(bf16[64,256]{1,0:T(8,128)(2,1)S(1)} %add_convert_fusion.5), channel_id=1, source_target_pairs={{0,4},{4,0},{8,12},{12,8},{16,20},{20,16},{24,28},{28,24},{32,36},... | collective-permute-start | bytes 98312 | tf_op jit(solution)/shard_map/ppermute | solution.py:24
  242.3 5.4 collective-permute-start.23
Sparse Core Ops, SparseCore 0:
  18.5 55.7 all-gather.1
  120.7 783.7 all-reduce.1
  907.8 49.4 reduce-scatter.1
where the time goes:
time: 978 us; the launch traced here: 967 us
  waiting for transfers between devices  710 us (73%)
  local copies, waits for them, and re-layouts  85.1 us (9%)
  matrix products  78.2 us (8%)
  starting transfers between devices  47.6 us (5%)
  other arithmetic  30 us (3%)
  between operations  15.6 us (2%)
    psum x1, waiting for transfers between devices, local(): weight_grad = lax.psum(weight_part, 'tile')  649 us
    reduce_scatter x1, waiting for transfers between devices, local(): lax.psum_scatter(terms.astype(jnp.bfloat16), 'head', scatter_dimension=1,...  52.8 us
    ppermute x24, starting transfers between devices, swapped(): return lax.ppermute(block, axis, route)  47.3 us
    broadcast_in_dim x24, local copies, waits for them, and re-layouts, local(): jnp.broadcast_to(entry[None], (tiles, POOLED, width))  25.5 us
    dot_general x1, matrix products, local(): jnp.einsum('thqk,tkhd->tqhd', dscore, key_all, preferred_element_type=jnp...  20.2 us
  transfers between devices with their start and end apart: 27, of which 12 were waited for; matrix products, arithmetic and copies ran while one was open for 19% of the time, Pallas kernels for 0%

commit v1 on v0

v1 whole, which is shorter than its diff:
```python
import math

import jax
import jax.numpy as jnp
from jax import lax
from jax.experimental import pallas as pl
from jax.experimental.pallas import tpu as pltpu
from jax.sharding import PartitionSpec as P

BF = jnp.bfloat16
F32 = jnp.float32
MESH = pl.DeviceIdType.MESH
ROOT_HALF = 1.0 / math.sqrt(2.0)
NT = (((1,), (1,)), ((), ()))
TILE = 256
W = 256


def mm(a, b):
    return jnp.dot(a, b, preferred_element_type=F32)


def mm_nt(a, b):
    return lax.dot_general(a, b, NT, preferred_element_type=F32)


def iota(shape, axis):
    return lax.broadcasted_iota(jnp.int32, shape, axis)


def ones_where(mask):
    return jnp.where(mask, 1.0, 0.0).astype(BF)


def pool2(x):
    n = x.shape[0]
    pairs = ones_where((iota((n // 2, n), 1) >> 1) == iota((n // 2, n), 0))
    return (mm(pairs, x) * ROOT_HALF).astype(BF)


def repeat_rows(x, times_log2):
    n = x.shape[0]
    big = n << times_log2
    spread = ones_where((iota((big, n), 0) >> times_log2) == iota((big, n), 1))
    high = x.astype(BF)
    low = (x - high.astype(F32)).astype(BF)
    return mm(spread, high) + mm(spread, low)


def spread2(x):
    return repeat_rows(x, 1) * ROOT_HALF


def lanes(a, b):
    return jnp.concatenate([a, b], axis=1)


def stack_kv(x):
    return jnp.concatenate([x[:, :W], x[:, W:]], axis=0)


def unstack_kv(x):
    n = x.shape[0] // 2
    return jnp.concatenate([x[:n], x[n:]], axis=1)


def kernel(
    q_hbm, k_hbm, v_hbm, w_hbm, c_hbm,
    out_hbm, gq_hbm, gk_hbm, gv_hbm, wg_hbm,
    q_v, ks, vs, kst, vst, w_v, cot, pt_v, dst_v, mixt, mixf, mixed, ma, ob, outr, gq_v, gk_v, gv_v,
    qbd, gbd, dko, dvo, p0, p1, fg, wpart, ws, wr, ws2, wr2, wg3, wg4, wgo,
    u0, u1, u2, ru0, ru1, ru2, n3f, h0, h1, h2, rh0, rh1, rh2, fk, fv,
    e0, e1, e2, e3, e4, e5, re0, re1, re2, re3, re4, re5, d3s, rd3,
    in_sem, out_sem, ag_send, ag_recv, up_send, up_recv, uh_send, uh_recv,
    ma_send, ma_recv, ob_send, ob_recv,
    w1_send, w1_recv, w2_send, w2_recv, w3_send, w3_recv, w4_send, w4_recv,
    dl_send, dl_recv, dh_send, dh_recv, d3_send, d3_recv,
):
    pos = lax.axis_index("tile")
    h = lax.axis_index("head")
    i = pos & 7
    g = pos >> 3

    in_cot = [pltpu.make_async_copy(c_hbm.at[c], cot.at[h, c], in_sem.at[c]) for c in range(4)]
    in_k = [pltpu.make_async_copy(k_hbm.at[t], ks.at[t, pl.ds(0, TILE)], in_sem.at[4 + t]) for t in range(4)]
    in_v = [pltpu.make_async_copy(v_hbm.at[t], vs.at[t, pl.ds(0, TILE)], in_sem.at[8 + t]) for t in range(4)]
    in_q = pltpu.make_async_copy(q_hbm, q_v, in_sem.at[12])
    in_w = pltpu.make_async_copy(w_hbm, w_v, in_sem.at[13])
    for copy in in_k + in_v + in_cot + [in_q, in_w]:
        copy.start()

    barrier = pltpu.get_barrier_semaphore()
    for m in range(1, 8):
        pl.semaphore_signal(barrier, inc=1, device_id=(pos ^ m, h), device_id_type=MESH)
        pl.semaphore_signal(barrier, inc=1, device_id=(pos ^ (8 * m), h), device_id_type=MESH)
    for m in range(1, 4):
        pl.semaphore_signal(barrier, inc=1, device_id=(pos, h ^ m), device_id_type=MESH)
    pl.semaphore_wait(barrier, 17)

    def remote(src, dst, send_sem, recv_sem, to_pos, to_head):
        return pltpu.make_async_remote_copy(
            src_ref=src, dst_ref=dst, send_sem=send_sem, recv_sem=recv_sem,
            device_id=(to_pos, to_head), device_id_type=MESH,
        )

    def ag_right(k, c):
        return remote(cot.at[h - k, c], cot.at[h - k, c], ag_send.at[0, k, c], ag_recv.at[0, k, c], pos, h + 1)

    def ag_left(k, c):
        return remote(cot.at[h + k, c], cot.at[h + k, c], ag_send.at[1, k, c], ag_recv.at[1, k, c], pos, h - 1)

    def ag_wait_right(k, c):
        remote(cot.at[h - k, c], cot.at[h - k, c], ag_send.at[0, k - 1, c], ag_recv.at[0, k - 1, c], pos, h).wait_recv()

    def ag_wait_left(k, c):
        remote(cot.at[h + k, c], cot.at[h + k, c], ag_send.at[1, k - 1, c], ag_recv.at[1, k - 1, c], pos, h).wait_recv()

    def ag_forward(k, c):
        @pl.when(h - k >= 0)
        def _():
            ag_wait_right(k, c)

            @pl.when(h < 3)
            def _():
                ag_right(k, c).start()

        @pl.when(h + k <= 3)
        def _():
            ag_wait_left(k, c)

            @pl.when(h > 0)
            def _():
                ag_left(k, c).start()

    for copy in in_k + in_v:
        copy.wait()
    quads = ones_where((iota((64, TILE), 1) >> 2) == iota((64, TILE), 0))
    leaf = [
        (mm(quads, lanes(ks[t, 0:TILE, :], vs[t, 0:TILE, :])) * 0.5).astype(BF) for t in range(4)
    ]
    node1 = [pool2(jnp.concatenate([leaf[2 * n], leaf[2 * n + 1]], axis=0)) for n in range(2)]
    top = pool2(jnp.concatenate(node1, axis=0))
    pool_1 = pool2(top)
    pool_2 = pool2(pool_1)
    n = 16
    pairs = ones_where((iota((n // 2, n), 1) >> 1) == iota((n // 2, n), 0))
    pool_3f = (mm(pairs, pool_2) * ROOT_HALF).astype(BF).astype(F32)
    pool_3 = jnp.concatenate([pool_3f[:, :W], pool_3f[:, W:]], axis=0).astype(BF)
    u0[0:128, :] = stack_kv(top)
    u0[128:144, :] = pool_3
    u1[0:64, :] = stack_kv(pool_1)
    u1[64:80, :] = pool_3
    u2[0:32, :] = stack_kv(pool_2)
    u2[32:48, :] = pool_3

    def low_pair(m, s0, r0, s1, r1, s2, r2):
        if m == 1:
            return s0, r0
        if m < 4:
            return s1, r1.at[m - 2]
        return s2, r2.at[m - 4]

    up = []
    for m in range(1, 8):
        src, dst = low_pair(m, u0, ru0, u1, ru1, u2, ru2)
        up.append(remote(src, dst, up_send.at[m - 1], up_recv.at[m - 1], pos ^ m, h))
        up[-1].start()

    for copy in in_cot:
        copy.wait()
    for c in range(4):
        @pl.when(h < 3)
        def _():
            ag_right(0, c).start()

        @pl.when(h > 0)
        def _():
            ag_left(0, c).start()

    for t in range(4):
        other = leaf[t ^ 1]
        ks[t, 256:320, :] = other[:, :W]
        vs[t, 256:320, :] = other[:, W:]
        other = node1[(t >> 1) ^ 1]
        ks[t, 320:384, :] = other[:, :W]
        vs[t, 320:384, :] = other[:, W:]
        kst[t, :, 0:384] = ks[t, 0:384, :].T
        vst[t, :, 0:384] = vs[t, 0:384, :].T

    in_q.wait()
    in_w.wait()

    n3f[pl.ds(pl.multiple_of(i * 8, 8), 8), :] = jnp.concatenate([pool_3f[:, :W], pool_3f[:, W:]], axis=1)

    def put_group_part(part, sender):
        part = part.astype(F32)
        n3f[pl.ds(pl.multiple_of(sender * 8, 8), 8), :] = jnp.concatenate([part[0:8], part[8:16]], axis=1)

    for m in range(1, 8):
        up[m - 1].wait_recv()
        sender = i ^ m
        if m == 1:
            fk[0:64, :] = ru0[0:64, :]
            fv[0:64, :] = ru0[64:128, :]
            put_group_part(ru0[128:144, :], sender)
        elif m < 4:
            at = pl.multiple_of(64 + (sender & 1) * 32, 32)
            fk[pl.ds(at, 32), :] = ru1[m - 2, 0:32, :]
            fv[pl.ds(at, 32), :] = ru1[m - 2, 32:64, :]
            put_group_part(ru1[m - 2, 64:80, :], sender)
        else:
            at = pl.multiple_of(128 + (sender & 3) * 16, 16)
            fk[pl.ds(at, 16), :] = ru2[m - 4, 0:16, :]
            fv[pl.ds(at, 16), :] = ru2[m - 4, 16:32, :]
            put_group_part(ru2[m - 4, 32:48, :], sender)
    group_node = n3f[...].astype(BF)
    group_1 = pool2(group_node)
    group_2 = pool2(group_1)
    h0[...] = stack_kv(group_node)
    h1[...] = stack_kv(group_1)
    h2[...] = stack_kv(group_2)
    uh = []
    for m in range(1, 8):
        src, dst = low_pair(m, h0, rh0, h1, rh1, h2, rh2)
        uh.append(remote(src, dst, uh_send.at[m - 1], uh_recv.at[m - 1], pos ^ (8 * m), h))
        uh[-1].start()

    for c in range(4):
        ag_forward(1, c)

    for m in range(1, 8):
        uh[m - 1].wait_recv()
        sender = g ^ m
        if m == 1:
            fk[192:256, :] = rh0[0:64, :]
            fv[192:256, :] = rh0[64:128, :]
        elif m < 4:
            at = pl.multiple_of(256 + (sender & 1) * 32, 32)
            fk[pl.ds(at, 32), :] = rh1[m - 2, 0:32, :]
            fv[pl.ds(at, 32), :] = rh1[m - 2, 32:64, :]
        else:
            at = pl.multiple_of(320 + (sender & 3) * 16, 16)
            fk[pl.ds(at, 16), :] = rh2[m - 4, 0:16, :]
            fv[pl.ds(at, 16), :] = rh2[m - 4, 16:32, :]
    far_kt = fk[...].T
    far_vt = fv[...].T
    for t in range(4):
        ks[t, 384:768, :] = fk[...]
        vs[t, 384:768, :] = fv[...]
        kst[t, :, 384:768] = far_kt
        vst[t, :, 384:768] = far_vt

    head_masks = [ones_where((iota((TILE, W), 1) >> 6) == hd) for hd in range(4)]

    def forward(step, carry):
        t = (step + h + 1) & 3
        q_tile = q_v[t] * jnp.asarray(0.125, BF)
        for hd in range(4):
            scores = mm_nt(ks[t], q_tile * head_masks[hd])
            peak = jnp.max(scores, axis=0, keepdims=True)
            weights = jnp.exp(scores - peak)
            total = jnp.sum(weights, axis=0, keepdims=True)
            probs = (weights * (1.0 / total)).astype(BF)
            pt_v[t, :, hd * 256:(hd + 1) * 256] = probs
            mixf[t, hd * 64:(hd + 1) * 64, :] = mm(vst[t, hd * 64:(hd + 1) * 64, :], probs)
        whole = mixf[t]
        mixt[t] = whole.astype(BF)
        mixed[t] = whole.T.astype(BF)

        @pl.when(t != h)
        def _():
            remote(mixed.at[t], ma.at[h], ma_send.at[t], ma_recv.at[h], pos, t).start()

        @pl.when(t == h)
        def _():
            ma[h] = mixed[t]

        @pl.when(step >= 2)
        def _():
            ag_forward(2, 2 * step - 4)
            ag_forward(2, 2 * step - 3)

        return carry

    lax.fori_loop(0, 4, forward, 0)

    w1 = [
        remote(ws.at[i ^ m], wr.at[m], w1_send.at[m - 1], w1_recv.at[m - 1], pos ^ m, h)
        for m in range(1, 8)
    ]
    own_rows = pl.ds(pl.multiple_of(h * W, W), W)
    wpart[...] = jnp.zeros_like(wpart)
    fg[...] = jnp.zeros_like(fg)

    def backward(t, carry):
        @pl.when(h == 3)
        def _():
            ag_wait_right(3, t)

        @pl.when(h == 0)
        def _():
            ag_wait_left(3, t)

        gmt = mm_nt(w_v[own_rows, 0:W], cot[0, t])
        for s in range(1, 4):
            gmt = gmt + mm_nt(w_v[own_rows, s * W:(s + 1) * W], cot[s, t])
        for s in range(4):
            wpart[:, s * W:(s + 1) * W] += mm(mixt[t], cot[s, t])

        @pl.when(t == 3)
        def _():
            for r in range(8):
                ws[r] = wpart[r * 32:(r + 1) * 32, :].astype(BF)
            for copy in w1:
                copy.start()

        gm = gmt.T.astype(BF)
        gmt = gmt.astype(BF).astype(F32)
        q_tile = q_v[t] * jnp.asarray(0.125, BF)
        dqt = []
        for hd in range(4):
            at = slice(hd * 64, (hd + 1) * 64)
            block = slice(hd * 256, (hd + 1) * 256)
            gm_head = gm * head_masks[hd]
            gbd[block, :] = gm_head
            qbd[block, :] = q_tile * head_masks[hd]
            centre = jnp.sum(gmt[at] * mixf[t, at, :], axis=0, keepdims=True)
            grad_probs = mm_nt(vs[t], gm_head)
            dscore = (pt_v[t, :, block].astype(F32) * (grad_probs - centre)).astype(BF)
            dst_v[:, block] = dscore
            dqt.append(mm(kst[t, at, :], dscore))
        gq_v[t] = (jnp.concatenate(dqt, axis=0) * 0.125).T.astype(BF)
        pltpu.make_async_copy(gq_v.at[t], gq_hbm.at[t], out_sem.at[t]).start()
        dk = mm(dst_v[...], qbd[...])
        dv = mm(pt_v[t], gbd[...])
        dko[t] = dk[0:256]
        dvo[t] = dv[0:256]
        p0[t] = lanes(dk[256:320], dv[256:320])
        p1[t] = lanes(dk[320:384], dv[320:384])
        fg[...] += lanes(dk[384:768], dv[384:768])
        return carry

    lax.fori_loop(0, 4, backward, 0)

    def level(b):
        return fg[b * 64:(b + 1) * 64, :]

    def cut(buffer, b, parts):
        rows = 64 // parts
        whole = level(b)
        for part in range(parts):
            buffer[part] = stack_kv(whole[part * rows:(part + 1) * rows]).astype(BF)

    e3[...] = stack_kv(level(3)).astype(BF)
    cut(e4, 4, 2)
    cut(e5, 5, 4)

    def down_pair(m, index, s0, r0, s1, r1, s2, r2):
        if m == 1:
            return s0, r0
        if m < 4:
            return s1.at[(index ^ m) & 1], r1.at[m - 2]
        return s2.at[(index ^ m) & 3], r2.at[m - 4]

    dh = []
    for m in range(1, 8):
        src, dst = down_pair(m, g, e3, re3, e4, re4, e5, re5)
        dh.append(remote(src, dst, dh_send.at[m - 1], dh_recv.at[m - 1], pos ^ (8 * m), h))
        dh[-1].start()
    e0[...] = stack_kv(level(0)).astype(BF)
    cut(e1, 1, 2)
    cut(e2, 2, 4)
    dl = []
    for m in range(1, 8):
        src, dst = down_pair(m, i, e0, re0, e1, re1, e2, re2)
        dl.append(remote(src, dst, dl_send.at[m - 1], dl_recv.at[m - 1], pos ^ m, h))
        dl[-1].start()

    for copy in w1:
        copy.wait_recv()
    total = wpart[pl.ds(pl.multiple_of(i * 32, 32), 32), :]
    for m in range(1, 8):
        total = total + wr[m].astype(F32)
    for r in range(8):
        ws2[r] = total[:, r * 128:(r + 1) * 128].astype(BF)
    w2 = []
    for m in range(1, 8):
        w2.append(remote(ws2.at[g ^ m], wr2.at[m], w2_send.at[m - 1], w2_recv.at[m - 1], pos ^ (8 * m), h))
        w2[-1].start()

    for m in range(1, 4):
        remote(ma.at[h ^ m], ma.at[h ^ m], ma_send.at[h ^ m], ma_recv.at[h ^ m], pos, h).wait_recv()
    to_heads = []
    for c in range(4):
        block = mm(ma[0], w_v[0:W, c * W:(c + 1) * W])
        for s in range(1, 4):
            block = block + mm(ma[s], w_v[s * W:(s + 1) * W, c * W:(c + 1) * W])
        ob[c] = block.astype(BF)
    for m in range(1, 4):
        to_heads.append(
            remote(ob.at[h ^ m], outr.at[m], ob_send.at[m - 1], ob_recv.at[m - 1], pos, h ^ m)
        )
        to_heads[-1].start()
    own_out = pltpu.make_async_copy(ob.at[h], out_hbm.at[h], out_sem.at[4])
    own_out.start()

    for copy in dh:
        copy.wait_recv()

    def f32_kv(x):
        return unstack_kv(x.astype(F32))

    quarter = f32_kv(re5[0]) + f32_kv(re5[1]) + f32_kv(re5[2]) + f32_kv(re5[3])
    half = f32_kv(re4[0]) + f32_kv(re4[1]) + spread2(quarter)
    group_grad = f32_kv(re3[...]) + spread2(half)
    for r in range(8):
        d3s[r] = stack_kv(group_grad[r * 8:(r + 1) * 8]).astype(BF)
    d3 = []
    for m in range(1, 8):
        d3.append(remote(d3s.at[i ^ m], rd3.at[m], d3_send.at[m - 1], d3_recv.at[m - 1], pos ^ m, h))
        d3[-1].start()

    for copy in w2:
        copy.wait_recv()
    block = ws2[g].astype(F32)
    for m in range(1, 8):
        block = block + wr2[m].astype(F32)
    wg3[g] = block.astype(BF)
    w3 = []
    for m in range(1, 8):
        w3.append(remote(wg3.at[g], wg3.at[g], w3_send.at[m - 1], w3_recv.at[m - 1], pos ^ (8 * m), h))
        w3[-1].start()

    for copy in dl:
        copy.wait_recv()
    for copy in d3:
        copy.wait_recv()
    eighth = f32_kv(d3s[i])
    for m in range(1, 8):
        eighth = eighth + f32_kv(rd3[m])
    quarter = f32_kv(re2[0]) + f32_kv(re2[1]) + f32_kv(re2[2]) + f32_kv(re2[3]) + spread2(eighth)
    half = f32_kv(re1[0]) + f32_kv(re1[1]) + spread2(quarter)
    top_grad = f32_kv(re0[...]) + spread2(half)
    spread_top = spread2(top_grad)
    for n in range(2):
        first = 2 * (1 - n)
        down_1 = p1[first] + p1[first + 1] + spread_top[n * 64:(n + 1) * 64]
        spread_1 = spread2(down_1)
        for r in range(2):
            t = 2 * n + r
            down_0 = p0[t ^ 1] + spread_1[r * 64:(r + 1) * 64]
            back = repeat_rows(down_0, 2) * 0.5
            gk_v[t] = (dko[t] + back[:, :W]).astype(BF)
            gv_v[t] = (dvo[t] + back[:, W:]).astype(BF)
    out_k = pltpu.make_async_copy(gk_v, gk_hbm, out_sem.at[5])
    out_v = pltpu.make_async_copy(gv_v, gv_hbm, out_sem.at[6])
    out_k.start()
    out_v.start()

    for m in range(1, 8):
        remote(wg3.at[g ^ m], wg3.at[g ^ m], w3_send.at[m - 1], w3_recv.at[m - 1], pos, h).wait_recv()
    w4 = []
    for m in range(1, 8):
        w4.append(remote(wg3, wg4.at[m], w4_send.at[m - 1], w4_recv.at[m - 1], pos ^ m, h))
        w4[-1].start()

    out_parts = []
    for m in range(1, 4):
        to_heads[m - 1].wait_recv()
        out_parts.append(pltpu.make_async_copy(outr.at[m], out_hbm.at[h ^ m], out_sem.at[6 + m]))
        out_parts[-1].start()

    def put_rows(owner, blocks):
        rows = pl.ds(pl.multiple_of(owner * 32, 32), 32)
        for r in range(8):
            wgo[rows, r * 128:(r + 1) * 128] = blocks[r].astype(F32)

    put_rows(i, wg3[...])
    for m in range(1, 8):
        w4[m - 1].wait_recv()
        put_rows(i ^ m, wg4[m])
    out_w = pltpu.make_async_copy(wgo, wg_hbm, out_sem.at[10])
    out_w.start()

    for copy in up + uh + w1 + w2 + w3 + w4 + dl + dh + d3 + to_heads:
        copy.wait_send()
    for m in range(1, 4):
        t = h ^ m
        remote(mixed.at[t], ma.at[h], ma_send.at[t], ma_recv.at[h], pos, t).wait_send()
    for k in range(3):
        for c in range(4):
            @pl.when(jnp.logical_and(h - k >= 0, h < 3))
            def _():
                ag_right(k, c).wait_send()

            @pl.when(jnp.logical_and(h + k <= 3, h > 0))
            def _():
                ag_left(k, c).wait_send()
    for t in range(4):
        pltpu.make_async_copy(gq_v.at[t], gq_hbm.at[t], out_sem.at[t]).wait()
    for copy in [own_out, out_k, out_v, out_w] + out_parts:
        copy.wait()


def local(queries, keys, values, out_weight, cotangent):
    tiles = (4, TILE, W)
    any_space = pl.BlockSpec(memory_space=pl.ANY)

    def v(*shape, dtype=BF):
        return pltpu.VMEM(shape, dtype)

    def f(*shape):
        return pltpu.VMEM(shape, F32)

    dma = pltpu.SemaphoreType.DMA
    scratch = [
        v(4, 256, 256), v(4, 768, 256), v(4, 768, 256), v(4, 256, 768), v(4, 256, 768),
        v(1024, 1024), v(4, 4, 256, 256), v(4, 768, 1024), v(768, 1024),
        v(4, 256, 256), f(4, 256, 256), v(4, 256, 256), v(4, 256, 256),
        v(4, 256, 256), v(4, 256, 256), v(4, 256, 256), v(4, 256, 256), v(4, 256, 256),
        v(1024, 256), v(1024, 256), f(4, 256, 256), f(4, 256, 256),
        f(4, 64, 512), f(4, 64, 512), f(384, 512), f(256, 1024),
        v(8, 32, 1024), v(8, 32, 1024), v(8, 32, 128), v(8, 32, 128),
        v(8, 32, 128), v(8, 8, 32, 128), f(256, 1024),
        v(144, 256), v(80, 256), v(48, 256), v(144, 256), v(2, 80, 256), v(4, 48, 256),
        f(64, 512), v(128, 256), v(64, 256), v(32, 256),
        v(128, 256), v(2, 64, 256), v(4, 32, 256), v(384, 256), v(384, 256),
        v(128, 256), v(2, 64, 256), v(4, 32, 256), v(128, 256), v(2, 64, 256), v(4, 32, 256),
        v(128, 256), v(2, 64, 256), v(4, 32, 256), v(128, 256), v(2, 64, 256), v(4, 32, 256),
        v(8, 16, 256), v(8, 16, 256),
        dma((14,)), dma((11,)), dma((2, 3, 4)), dma((2, 3, 4)),
        dma((7,)), dma((7,)), dma((7,)), dma((7,)),
        dma((4,)), dma((4,)), dma((3,)), dma((3,)),
    ] + [dma((7,))] * 8 + [dma((7,))] * 6
    out_shape = [jax.ShapeDtypeStruct(tiles, BF)] * 4 + [jax.ShapeDtypeStruct((256, 1024), F32)]
    output, gq, gk, gv, wg = pl.pallas_call(
        kernel,
        out_shape=out_shape,
        in_specs=[any_space] * 5,
        out_specs=[any_space] * 5,
        scratch_shapes=scratch,
        compiler_params=pltpu.CompilerParams(
            collective_id=0, has_side_effects=True, vmem_limit_bytes=60 * 1024 * 1024
        ),
    )(
        queries.reshape(tiles), keys.reshape(tiles), values.reshape(tiles), out_weight,
        cotangent.reshape(tiles),
    )
    rows = queries.shape
    return output.reshape(rows), gq.reshape(rows), gk.reshape(rows), gv.reshape(rows), wg


def solution(mesh):
    in_specs = (P("tile", "head"), P("tile", "head"), P("tile", "head"), P(), P("tile", "head"))
    out_specs = (
        P("tile", "head"),
        P("tile", "head"),
        P("tile", "head"),
        P("tile", "head"),
        P("head", None),
    )
    return jax.shard_map(local, mesh=mesh, in_specs=in_specs, out_specs=out_specs, check_vma=False)
```

time: 978 us -> 102 us (0.10); the launches traced: 967 us -> 101 us
  waiting for transfers between devices: 710 us -> 0 us
  Pallas kernels: 0 us -> 94.3 us
  local copies, waits for them, and re-layouts: 85.1 us -> 6.45 us
  matrix products: 78.2 us -> 0 us
  starting transfers between devices: 47.6 us -> 0 us
  other arithmetic: 30 us -> 0 us
  between operations: 15.6 us -> 0.67 us
    psum x1 -> x0, waiting for transfers between devices: 649 us -> none  [local(): weight_grad = lax.psum(weight_part, 'tile')]
    pallas_call x0 -> x1, Pallas kernels: none -> 94.3 us  [local(): pl.pallas_call(kernel, out_shape=out_shape, in_specs=[any_space] * 5, out...]
    dot_general x8 -> x0, matrix products: 67.9 us -> none  [the longest x1 20.2 us: local(): jnp.einsum('thqk,tkhd->tqhd', dscore, key_all, preferred_element_type=jnp...]
    reduce_scatter x1 -> x0, waiting for transfers between devices: 52.8 us -> none  [local(): lax.psum_scatter(terms.astype(jnp.bfloat16), 'head', scatter_dimension=1,...]
    ppermute x24 -> x0, starting transfers between devices: 47.3 us -> none  [swapped(): return lax.ppermute(block, axis, route)]
    broadcast_in_dim x54 -> x0, local copies, waits for them, and re-layouts: 28.2 us -> none  [the longest x24 25.5 us: local(): jnp.broadcast_to(entry[None], (tiles, POOLED, width))]
    concatenate x6 -> x0, local copies, waits for them, and re-layouts: 15.9 us -> none  [the longest x3 8.79 us: local(): jnp.concatenate([values.reshape(tiles, TILE, width)] + far_v, axis=1)]
    convert_element_type x38 -> x0, other arithmetic: 15.4 us -> none  [the longest x5 4.25 us: local(): level_k.astype(jnp.bfloat16)]
  transfers between devices with their start and end apart: 27 -> 0, of which waited for: 12 -> 0; matrix products, arithmetic and copies ran while one was open for 19% -> 0% of each run, Pallas kernels for 0% -> 0%
where the time goes in v1:
time: 102 us; the launch traced here: 101 us
  Pallas kernels  94.3 us (92%)
  local copies, waits for them, and re-layouts  6.45 us (6%)
    pallas_call x1, Pallas kernels, local(): pl.pallas_call(kernel, out_shape=out_shape, in_specs=[any_space] * 5, out...  94.3 us
    unnamed x11, local copies, waits for them, and re-layouts  6.45 us

profile of v1, /device:TPU:1, one launch (start us, length us, event | category | flops | bytes accessed | tf_op | source)
XLA Modules:
  0.0 101.4 jit_solution(18434939451147018861)
XLA Ops:
  0.6 94.3 %shard_map.92 = (bf16[4,256,256]{2,1,0:T(8,128)(2,1)}, bf16[4,256,256]{2,1,0:T(8,128)(2,1)}, bf16[4,256,256]{2,1,0:T(8,128)(2,1)}, bf16[4,256,256]{2,1,0:T(8,128)(2,1)}, f32[256,1024]{1,0:T(8,128)}) custom-call(bf16[4,256,256]{2,1,0:T(8,128)(2,1)} %bitcast.12, bf16[4,256,256]{2,1,0:T(8,128)(2,1)} %bitcast.13, bf16[4,256,256]{2,1,0:T(8,128)(2,1)} %bitcast.14, ...), custom_call_target="tpu_custom_call" | custom-call | tf_op jit(solution)/shard_map/pallas_call | solution.py:536
  94.9 0.0 copy-start.2
  94.9 0.0 copy-start.1
  94.9 0.0 copy-start
  94.9 2.0 %copy.15 = bf16[1024,256]{1,0:T(8,128)(2,1)} copy(bf16[1024,256]{1,0:T(8,128)(2,1)} %bitcast.11) | data formatting | bytes 1048576
  96.9 1.9 %copy.16 = bf16[1024,256]{1,0:T(8,128)(2,1)} copy(bf16[1024,256]{1,0:T(8,128)(2,1)} %bitcast.10) | data formatting | bytes 1048576
  98.8 0.0 copy-done.2
  98.8 0.8 copy.17
  99.6 0.0 copy-done.1
  99.6 0.8 copy.18
  100.4 0.0 copy-done
  100.4 1.0 copy.19
Async XLA Ops:
  94.9 3.9 %copy-start.2 = (bf16[4,256,256]{2,1,0:T(8,128)(2,1)S(1)}, bf16[4,256,256]{2,1,0:T(8,128)(2,1)}, u32[]{:S(2)}) copy-start(bf16[4,256,256]{2,1,0:T(8,128)(2,1)} %get-tuple-element.12) | copy-start | bytes 1572868
  94.9 4.7 %copy-start.1 = (bf16[4,256,256]{2,1,0:T(8,128)(2,1)S(1)}, bf16[4,256,256]{2,1,0:T(8,128)(2,1)}, u32[]{:S(2)}) copy-start(bf16[4,256,256]{2,1,0:T(8,128)(2,1)} %get-tuple-element.13) | copy-start | bytes 1572868
  94.9 5.5 %copy-start = (f32[256,1024]{1,0:T(8,128)S(1)}, f32[256,1024]{1,0:T(8,128)}, u32[]{:S(2)}) copy-start(f32[256,1024]{1,0:T(8,128)} %get-tuple-element.24) | copy-start | bytes 3145732

commit v2 on v1

--- a/solution.py
+++ b/solution.py
@@ -66,12 +66,13 @@
 
 def kernel(
     q_hbm, k_hbm, v_hbm, w_hbm, c_hbm,
-    out_hbm, gq_hbm, gk_hbm, gv_hbm, wg_hbm,
-    q_v, ks, vs, kst, vst, w_v, cot, pt_v, dst_v, mixt, mixf, mixed, ma, ob, outr, gq_v, gk_v, gv_v,
-    qbd, gbd, dko, dvo, p0, p1, fg, wpart, ws, wr, ws2, wr2, wg3, wg4, wgo,
+    outr, gq_v, gk_v, gv_v, wgo,
+    q_v, ks, vs, kst, vst, w_v, cot, pt_v, dst_v, mixt, mixf, mixed, ma, ob,
+    qbd, gbd, dko, dvo, p0, p1, fg, wpart, wsa, wra, ws2a, wr2a, wg3a, wg4a,
+    wsb, wrb, ws2b, wr2b, wg3b, wg4b,
     u0, u1, u2, ru0, ru1, ru2, n3f, h0, h1, h2, rh0, rh1, rh2, fk, fv,
     e0, e1, e2, e3, e4, e5, re0, re1, re2, re3, re4, re5, d3s, rd3,
-    in_sem, out_sem, ag_send, ag_recv, up_send, up_recv, uh_send, uh_recv,
+    in_sem, ag_send, ag_recv, up_send, up_recv, uh_send, uh_recv,
     ma_send, ma_recv, ob_send, ob_recv,
     w1_send, w1_recv, w2_send, w2_recv, w3_send, w3_recv, w4_send, w4_recv,
     dl_send, dl_recv, dh_send, dh_recv, d3_send, d3_recv,
@@ -90,12 +91,12 @@
         copy.start()
 
     barrier = pltpu.get_barrier_semaphore()
-    for m in range(1, 8):
-        pl.semaphore_signal(barrier, inc=1, device_id=(pos ^ m, h), device_id_type=MESH)
+    for m in (4, 5, 6, 7, 2, 3, 1):
         pl.semaphore_signal(barrier, inc=1, device_id=(pos ^ (8 * m), h), device_id_type=MESH)
     for m in range(1, 4):
         pl.semaphore_signal(barrier, inc=1, device_id=(pos, h ^ m), device_id_type=MESH)
-    pl.semaphore_wait(barrier, 17)
+    for m in range(1, 8):
+        pl.semaphore_signal(barrier, inc=1, device_id=(pos ^ m, h), device_id_type=MESH)
 
     def remote(src, dst, send_sem, recv_sem, to_pos, to_head):
         return pltpu.make_async_remote_copy(
@@ -153,6 +154,10 @@
     u2[0:32, :] = stack_kv(pool_2)
     u2[32:48, :] = pool_3
 
+    for copy in in_cot:
+        copy.wait()
+    pl.semaphore_wait(barrier, 17)
+
     def low_pair(m, s0, r0, s1, r1, s2, r2):
         if m == 1:
             return s0, r0
@@ -166,8 +171,6 @@
         up.append(remote(src, dst, up_send.at[m - 1], up_recv.at[m - 1], pos ^ m, h))
         up[-1].start()
 
-    for copy in in_cot:
-        copy.wait()
     for c in range(4):
         @pl.when(h < 3)
         def _():
@@ -252,8 +255,15 @@
 
     head_masks = [ones_where((iota((TILE, W), 1) >> 6) == hd) for hd in range(4)]
 
+    def send_mixed(t):
+        return remote(
+            mixed.at[t], ma.at[t & 1, h], ma_send.at[t], ma_recv.at[t & 1, h], pos, 1 + (t >> 1)
+        )
+
+    middle = jnp.logical_and(h > 0, h < 3)
+
     def forward(step, carry):
-        t = (step + h + 1) & 3
+        t = (step + 2 * (1 - (h >> 1))) & 3
         q_tile = q_v[t] * jnp.asarray(0.125, BF)
         for hd in range(4):
             scores = mm_nt(ks[t], q_tile * head_masks[hd])
@@ -267,29 +277,150 @@
         mixt[t] = whole.astype(BF)
         mixed[t] = whole.T.astype(BF)
 
-        @pl.when(t != h)
-        def _():
-            remote(mixed.at[t], ma.at[h], ma_send.at[t], ma_recv.at[h], pos, t).start()
-
-        @pl.when(t == h)
-        def _():
-            ma[h] = mixed[t]
-
-        @pl.when(step >= 2)
-        def _():
-            ag_forward(2, 2 * step - 4)
-            ag_forward(2, 2 * step - 3)
-
+        owner = 1 + (t >> 1)
+
+        @pl.when(h != owner)
+        def _():
+            send_mixed(t).start()
+
+        @pl.when(h == owner)
+        def _():
+            ma[t & 1, h] = mixed[t]
+
+        ag_forward(2, step)
         return carry
 
     lax.fori_loop(0, 4, forward, 0)
 
-    w1 = [
-        remote(ws.at[i ^ m], wr.at[m], w1_send.at[m - 1], w1_recv.at[m - 1], pos ^ m, h)
-        for m in range(1, 8)
-    ]
+    upper = h >> 1
+    order_a = (h, h ^ 1, 2 - upper)
+    order_b = (3 * (1 - upper),)
+
+    class Reduction:
+        def __init__(self, order, part, bufs):
+            self.order, self.part, self.nb = order, part, len(order)
+            self.ws, self.wr, self.ws2, self.wr2, self.wg3, self.wg4 = bufs
+            self.first = 0 if part == 0 else 3
+
+        def begin(self):
+            for j, s in enumerate(self.order):
+                block = mm(mixt[0], cot[s, 0])
+                for t in range(1, 4):
+                    block = block + mm(mixt[t], cot[s, t])
+                wpart[self.first + j] = block
+                for r in range(8):
+                    self.ws[r, :, j * W:(j + 1) * W] = block[r * 32:(r + 1) * 32].astype(BF)
+            for copy in self.low():
+                copy.start()
+
+        def low(self):
+            return [
+                remote(self.ws.at[i ^ m], self.wr.at[m], w1_send.at[self.part, m - 1], w1_recv.at[self.part, m - 1], pos ^ m, h)
+                for m in range(1, 8)
+            ]
+
+        def high(self):
+            return [
+                remote(self.ws2.at[(g ^ m) & 3], self.wr2.at[g], w2_send.at[self.part, m - 1], w2_recv.at[self.part, m - 1],
+                       pos ^ (8 * m), h)
+                for m in range(1, 8)
+            ]
+
+        def back_x(self):
+            return [
+                remote(self.wg3.at[g & 3], self.wg3.at[g & 3], w3_send.at[self.part, m - 1], w3_recv.at[self.part, m - 1],
+                       pos ^ (8 * m), h)
+                for m in range(1, 4)
+            ]
+
+        def back_low(self):
+            return [
+                remote(self.wg3, self.wg4.at[m], w4_send.at[self.part, m - 1], w4_recv.at[self.part, m - 1], pos ^ m, h)
+                for m in range(1, 8)
+            ]
+
+        def to_high(self):
+            for copy in self.low():
+                copy.wait_recv()
+            half = self.nb * 128
+            rows = pl.ds(pl.multiple_of(i * 32, 32), 32)
+            total = jnp.concatenate([wpart[self.first + j, rows, :] for j in range(self.nb)], axis=1)
+            for m in range(1, 8):
+                total = total + self.wr[m].astype(F32)
+            for r in range(4):
+                piece = total[r * 8:(r + 1) * 8]
+                self.ws2[r] = jnp.concatenate([piece[:, :half], piece[:, half:]], axis=0).astype(BF)
+            for copy in self.high():
+                copy.start()
+            self.wr2[g] = self.ws2[g & 3]
+
+        def to_back_x(self):
+            for m in range(1, 8):
+                remote(self.ws2.at[0], self.wr2.at[g ^ m], w2_send.at[self.part, m - 1], w2_recv.at[self.part, m - 1], pos, h).wait_recv()
+            total = self.wr2[0].astype(F32)
+            for r in range(1, 8):
+                total = total + self.wr2[r].astype(F32)
+            self.wg3[g & 3] = total.astype(BF)
+            for copy in self.back_x():
+                copy.start()
+
+        def to_back_low(self):
+            for m in range(1, 4):
+                slot = self.wg3.at[(g ^ m) & 3]
+                remote(slot, slot, w3_send.at[self.part, m - 1], w3_recv.at[self.part, m - 1], pos, h).wait_recv()
+            for copy in self.back_low():
+                copy.start()
+            self.wg4[0] = self.wg3[...]
+
+        def finish(self):
+            for copy in self.back_low():
+                copy.wait_recv()
+            half = self.nb * 128
+
+            def put(m, carry):
+                for r in range(4):
+                    rows = pl.ds(pl.multiple_of((i ^ m) * 32 + r * 8, 8), 8)
+                    piece = self.wg4[m, r].astype(F32)
+                    for c in range(2 * self.nb):
+                        top, lane = (c * 128) // half, (c * 128) % half
+                        columns = pl.ds(pl.multiple_of(self.order[c // 2] * W + (c % 2) * 128, 128), 128)
+                        wgo[rows, columns] = piece[top * 8:(top + 1) * 8, lane:lane + 128]
+                return carry
+
+            lax.fori_loop(0, 8, put, 0)
+
+        def wait_sends(self):
+            for copy in self.low() + self.high() + self.back_x() + self.back_low():
+                copy.wait_send()
+
+    part_a = Reduction(order_a, 0, (wsa, wra, ws2a, wr2a, wg3a, wg4a))
+    part_b = Reduction(order_b, 1, (wsb, wrb, ws2b, wr2b, wg3b, wg4b))
+    part_a.begin()
+
+    def send_output(tile, c):
+        return remote(ob.at[tile, c], outr.at[2 * (h - 1) + tile], ob_send.at[tile, c], ob_recv.at[2 * (h - 1) + tile], pos, c)
+
+    def project():
+        for tile in range(2):
+            for s in range(4):
+                @pl.when(h != s)
+                def _():
+                    remote(ma.at[tile, s], ma.at[tile, s], ma_send.at[0], ma_recv.at[tile, s], pos, h).wait_recv()
+            for c in range(4):
+                block = mm(ma[tile, 0], w_v[0:W, c * W:(c + 1) * W])
+                for s in range(1, 4):
+                    block = block + mm(ma[tile, s], w_v[s * W:(s + 1) * W, c * W:(c + 1) * W])
+                ob[tile, c] = block.astype(BF)
+
+                @pl.when(h != c)
+                def _():
+                    send_output(tile, c).start()
+
+                @pl.when(h == c)
+                def _():
+                    outr[2 * (h - 1) + tile] = ob[tile, c]
+
     own_rows = pl.ds(pl.multiple_of(h * W, W), W)
-    wpart[...] = jnp.zeros_like(wpart)
     fg[...] = jnp.zeros_like(fg)
 
     def backward(t, carry):
@@ -304,15 +435,13 @@
         gmt = mm_nt(w_v[own_rows, 0:W], cot[0, t])
         for s in range(1, 4):
             gmt = gmt + mm_nt(w_v[own_rows, s * W:(s + 1) * W], cot[s, t])
-        for s in range(4):
-            wpart[:, s * W:(s + 1) * W] += mm(mixt[t], cot[s, t])
+        @pl.when(t == 2)
+        def _():
+            part_a.to_high()
 
         @pl.when(t == 3)
         def _():
-            for r in range(8):
-                ws[r] = wpart[r * 32:(r + 1) * 32, :].astype(BF)
-            for copy in w1:
-                copy.start()
+            part_b.begin()
 
         gm = gmt.T.astype(BF)
         gmt = gmt.astype(BF).astype(F32)
@@ -330,7 +459,6 @@
             dst_v[:, block] = dscore
             dqt.append(mm(kst[t, at, :], dscore))
         gq_v[t] = (jnp.concatenate(dqt, axis=0) * 0.125).T.astype(BF)
-        pltpu.make_async_copy(gq_v.at[t], gq_hbm.at[t], out_sem.at[t]).start()
         dk = mm(dst_v[...], qbd[...])
         dv = mm(pt_v[t], gbd[...])
         dko[t] = dk[0:256]
@@ -376,33 +504,14 @@
         dl.append(remote(src, dst, dl_send.at[m - 1], dl_recv.at[m - 1], pos ^ m, h))
         dl[-1].start()
 
-    for copy in w1:
-        copy.wait_recv()
-    total = wpart[pl.ds(pl.multiple_of(i * 32, 32), 32), :]
-    for m in range(1, 8):
-        total = total + wr[m].astype(F32)
-    for r in range(8):
-        ws2[r] = total[:, r * 128:(r + 1) * 128].astype(BF)
-    w2 = []
-    for m in range(1, 8):
-        w2.append(remote(ws2.at[g ^ m], wr2.at[m], w2_send.at[m - 1], w2_recv.at[m - 1], pos ^ (8 * m), h))
-        w2[-1].start()
-
-    for m in range(1, 4):
-        remote(ma.at[h ^ m], ma.at[h ^ m], ma_send.at[h ^ m], ma_recv.at[h ^ m], pos, h).wait_recv()
-    to_heads = []
-    for c in range(4):
-        block = mm(ma[0], w_v[0:W, c * W:(c + 1) * W])
-        for s in range(1, 4):
-            block = block + mm(ma[s], w_v[s * W:(s + 1) * W, c * W:(c + 1) * W])
-        ob[c] = block.astype(BF)
-    for m in range(1, 4):
-        to_heads.append(
-            remote(ob.at[h ^ m], outr.at[m], ob_send.at[m - 1], ob_recv.at[m - 1], pos, h ^ m)
-        )
-        to_heads[-1].start()
-    own_out = pltpu.make_async_copy(ob.at[h], out_hbm.at[h], out_sem.at[4])
-    own_out.start()
+    part_a.to_back_x()
+
+    @pl.when(middle)
+    def _():
+        project()
+
+    part_b.to_high()
+    part_a.to_back_low()
 
     for copy in dh:
         copy.wait_recv()
@@ -420,16 +529,7 @@
         d3.append(remote(d3s.at[i ^ m], rd3.at[m], d3_send.at[m - 1], d3_recv.at[m - 1], pos ^ m, h))
         d3[-1].start()
 
-    for copy in w2:
-        copy.wait_recv()
-    block = ws2[g].astype(F32)
-    for m in range(1, 8):
-        block = block + wr2[m].astype(F32)
-    wg3[g] = block.astype(BF)
-    w3 = []
-    for m in range(1, 8):
-        w3.append(remote(wg3.at[g], wg3.at[g], w3_send.at[m - 1], w3_recv.at[m - 1], pos ^ (8 * m), h))
-        w3[-1].start()
+    part_b.to_back_x()
 
     for copy in dl:
         copy.wait_recv()
@@ -452,41 +552,27 @@
             back = repeat_rows(down_0, 2) * 0.5
             gk_v[t] = (dko[t] + back[:, :W]).astype(BF)
             gv_v[t] = (dvo[t] + back[:, W:]).astype(BF)
-    out_k = pltpu.make_async_copy(gk_v, gk_hbm, out_sem.at[5])
-    out_v = pltpu.make_async_copy(gv_v, gv_hbm, out_sem.at[6])
-    out_k.start()
-    out_v.start()
-
-    for m in range(1, 8):
-        remote(wg3.at[g ^ m], wg3.at[g ^ m], w3_send.at[m - 1], w3_recv.at[m - 1], pos, h).wait_recv()
-    w4 = []
-    for m in range(1, 8):
-        w4.append(remote(wg3, wg4.at[m], w4_send.at[m - 1], w4_recv.at[m - 1], pos ^ m, h))
-        w4[-1].start()
-
-    out_parts = []
-    for m in range(1, 4):
-        to_heads[m - 1].wait_recv()
-        out_parts.append(pltpu.make_async_copy(outr.at[m], out_hbm.at[h ^ m], out_sem.at[6 + m]))
-        out_parts[-1].start()
-
-    def put_rows(owner, blocks):
-        rows = pl.ds(pl.multiple_of(owner * 32, 32), 32)
-        for r in range(8):
-            wgo[rows, r * 128:(r + 1) * 128] = blocks[r].astype(F32)
-
-    put_rows(i, wg3[...])
-    for m in range(1, 8):
-        w4[m - 1].wait_recv()
-        put_rows(i ^ m, wg4[m])
-    out_w = pltpu.make_async_copy(wgo, wg_hbm, out_sem.at[10])
-    out_w.start()
-
-    for copy in up + uh + w1 + w2 + w3 + w4 + dl + dh + d3 + to_heads:
+    part_b.to_back_low()
+    part_a.finish()
+    for t in range(4):
+        @pl.when(h != 1 + (t >> 1))
+        def _():
+            remote(outr.at[t], outr.at[t], ob_send.at[0, 0], ob_recv.at[t], pos, h).wait_recv()
+    part_b.finish()
+
+    for copy in up + uh + dl + dh + d3:
         copy.wait_send()
-    for m in range(1, 4):
-        t = h ^ m
-        remote(mixed.at[t], ma.at[h], ma_send.at[t], ma_recv.at[h], pos, t).wait_send()
+    part_a.wait_sends()
+    part_b.wait_sends()
+    for t in range(4):
+        @pl.when(h != 1 + (t >> 1))
+        def _():
+            send_mixed(t).wait_send()
+    for tile in range(2):
+        for c in range(4):
+            @pl.when(jnp.logical_and(middle, h != c))
+            def _():
+                send_output(tile, c).wait_send()
     for k in range(3):
         for c in range(4):
             @pl.when(jnp.logical_and(h - k >= 0, h < 3))
@@ -496,15 +582,30 @@
             @pl.when(jnp.logical_and(h + k <= 3, h > 0))
             def _():
                 ag_left(k, c).wait_send()
-    for t in range(4):
-        pltpu.make_async_copy(gq_v.at[t], gq_hbm.at[t], out_sem.at[t]).wait()
-    for copy in [own_out, out_k, out_v, out_w] + out_parts:
-        copy.wait()
+
+
+def hand_over(*arrays):
+    n = len(arrays)
+
+    def copy_kernel(*refs):
+        sems = refs[2 * n]
+        copies = [pltpu.make_async_copy(refs[k], refs[n + k], sems.at[k]) for k in range(n)]
+        for copy in copies:
+            copy.start()
+        for copy in copies:
+            copy.wait()
+
+    return pl.pallas_call(
+        copy_kernel,
+        out_shape=[jax.ShapeDtypeStruct(a.shape, a.dtype) for a in arrays],
+        in_specs=[pl.BlockSpec(memory_space=pltpu.VMEM)] * n,
+        out_specs=[pl.BlockSpec(memory_space=pltpu.HBM)] * n,
+        scratch_shapes=[pltpu.SemaphoreType.DMA((n,))],
+    )(*[pltpu.with_memory_space_constraint(a, pltpu.VMEM) for a in arrays])
 
 
 def local(queries, keys, values, out_weight, cotangent):
     tiles = (4, TILE, W)
-    any_space = pl.BlockSpec(memory_space=pl.ANY)
 
     def v(*shape, dtype=BF):
         return pltpu.VMEM(shape, dtype)
@@ -516,36 +617,40 @@
     scratch = [
         v(4, 256, 256), v(4, 768, 256), v(4, 768, 256), v(4, 256, 768), v(4, 256, 768),
         v(1024, 1024), v(4, 4, 256, 256), v(4, 768, 1024), v(768, 1024),
-        v(4, 256, 256), f(4, 256, 256), v(4, 256, 256), v(4, 256, 256),
-        v(4, 256, 256), v(4, 256, 256), v(4, 256, 256), v(4, 256, 256), v(4, 256, 256),
+        v(4, 256, 256), f(4, 256, 256), v(4, 256, 256), v(2, 4, 256, 256),
+        v(2, 4, 256, 256),
         v(1024, 256), v(1024, 256), f(4, 256, 256), f(4, 256, 256),
-        f(4, 64, 512), f(4, 64, 512), f(384, 512), f(256, 1024),
-        v(8, 32, 1024), v(8, 32, 1024), v(8, 32, 128), v(8, 32, 128),
-        v(8, 32, 128), v(8, 8, 32, 128), f(256, 1024),
+        f(4, 64, 512), f(4, 64, 512), f(384, 512), f(4, 256, 256),
+        v(8, 32, 768), v(8, 32, 768), v(4, 16, 384), v(8, 16, 384), v(4, 16, 384), v(8, 4, 16, 384),
+        v(8, 32, 256), v(8, 32, 256), v(4, 16, 128), v(8, 16, 128), v(4, 16, 128), v(8, 4, 16, 128),
         v(144, 256), v(80, 256), v(48, 256), v(144, 256), v(2, 80, 256), v(4, 48, 256),
         f(64, 512), v(128, 256), v(64, 256), v(32, 256),
         v(128, 256), v(2, 64, 256), v(4, 32, 256), v(384, 256), v(384, 256),
         v(128, 256), v(2, 64, 256), v(4, 32, 256), v(128, 256), v(2, 64, 256), v(4, 32, 256),
         v(128, 256), v(2, 64, 256), v(4, 32, 256), v(128, 256), v(2, 64, 256), v(4, 32, 256),
         v(8, 16, 256), v(8, 16, 256),
-        dma((14,)), dma((11,)), dma((2, 3, 4)), dma((2, 3, 4)),
+        dma((14,)), dma((2, 3, 4)), dma((2, 3, 4)),
         dma((7,)), dma((7,)), dma((7,)), dma((7,)),
-        dma((4,)), dma((4,)), dma((3,)), dma((3,)),
-    ] + [dma((7,))] * 8 + [dma((7,))] * 6
-    out_shape = [jax.ShapeDtypeStruct(tiles, BF)] * 4 + [jax.ShapeDtypeStruct((256, 1024), F32)]
+        dma((4,)), dma((2, 4)), dma((2, 4)), dma((4,)),
+    ] + [dma((2, 7))] * 8 + [dma((7,))] * 6
+    out_shape = [pltpu.VMEM(tiles, BF)] * 4 + [pltpu.VMEM((256, 1024), F32)]
     output, gq, gk, gv, wg = pl.pallas_call(
         kernel,
         out_shape=out_shape,
-        in_specs=[any_space] * 5,
-        out_specs=[any_space] * 5,
+        in_specs=[pl.BlockSpec(memory_space=pltpu.HBM)] * 5,
+        out_specs=[pl.BlockSpec(memory_space=pltpu.VMEM)] * 5,
         scratch_shapes=scratch,
         compiler_params=pltpu.CompilerParams(
-            collective_id=0, has_side_effects=True, vmem_limit_bytes=60 * 1024 * 1024
+            collective_id=0, has_side_effects=True, vmem_limit_bytes=48 * 1024 * 1024
         ),
-    )(
-        queries.reshape(tiles), keys.reshape(tiles), values.reshape(tiles), out_weight,
-        cotangent.reshape(tiles),
-    )
+    )(*[
+        pltpu.with_memory_space_constraint(a, pltpu.HBM)
+        for a in (
+            queries.reshape(tiles), keys.reshape(tiles), values.reshape(tiles), out_weight,
+            cotangent.reshape(tiles),
+        )
+    ])
+    output, gq, gk, gv, wg = hand_over(output, gq, gk, gv, wg)
     rows = queries.shape
     return output.reshape(rows), gq.reshape(rows), gk.reshape(rows), gv.reshape(rows), wg
 

time: 102 us -> 84.6 us (0.83)
  the two profiles are of different devices: /device:TPU:1 before, /device:TPU:33 now
where the time goes in v2:
time: 84.6 us; the launch traced here: 84.5 us
  Pallas kernels  83.9 us (99%)
    pallas_call x1, Pallas kernels, local(): pl.pallas_call(kernel, out_shape=out_shape, in_specs=[pl.BlockSpec(memory...  82.2 us
    pallas_call x1, Pallas kernels, hand_over(): pl.pallas_call(copy_kernel, out_shape=[jax.ShapeDtypeStruct(a.shape, a.dt...  1.71 us

profile of v2, /device:TPU:33, one launch (start us, length us, event | category | flops | bytes accessed | tf_op | source)
XLA Modules:
  0.0 84.5 jit_solution(7271119216405039199)
XLA Ops:
  0.6 82.2 %shard_map.92 = (bf16[4,256,256]{2,1,0:T(8,128)(2,1)S(1)}, bf16[4,256,256]{2,1,0:T(8,128)(2,1)S(1)}, bf16[4,256,256]{2,1,0:T(8,128)(2,1)S(1)}, bf16[4,256,256]{2,1,0:T(8,128)(2,1)S(1)}, f32[256,1024]{1,0:T(8,128)S(1)}) custom-call(bf16[4,256,256]{2,1,0:T(8,128)(2,1)} %bitcast.8, bf16[4,256,256]{2,1,0:T(8,128)(2,1)} %bitcast.9, ...), custom_call_target="tpu_custom_call" | custom-call | tf_op jit(solution)/shard_map/pallas_call | solution.py:637
  82.8 1.7 %shard_map.93 = (bf16[4,256,256]{2,1,0:T(8,128)(2,1)}, bf16[4,256,256]{2,1,0:T(8,128)(2,1)}, bf16[4,256,256]{2,1,0:T(8,128)(2,1)}, bf16[4,256,256]{2,1,0:T(8,128)(2,1)}, f32[256,1024]{1,0:T(8,128)}) custom-call(bf16[4,256,256]{2,1,0:T(8,128)(2,1)S(1)} %get-tuple-element.15.refs_0_, bf16[4,256,256]{2,1,0:T(8,128)(2,1)S(1)} %get-tuple-element.16.refs_1_, ...), custom_call_target="tpu_custom_call" | custom-call | tf_op jit(solution)/shard_map/pallas_call | solution.py:598

commit v3 on v2

--- a/solution.py
+++ b/solution.py
@@ -47,8 +47,12 @@
     return mm(spread, high) + mm(spread, low)
 
 
-def spread2(x):
-    return repeat_rows(x, 1) * ROOT_HALF
+def spread(x, levels):
+    return repeat_rows(x, levels) * ROOT_HALF ** levels
+
+
+def block(k):
+    return pl.ds(pl.multiple_of(k * W, W), W)
 
 
 def lanes(a, b):
@@ -67,8 +71,8 @@
 def kernel(
     q_hbm, k_hbm, v_hbm, w_hbm, c_hbm,
     outr, gq_v, gk_v, gv_v, wgo,
-    q_v, ks, vs, kst, vst, w_v, cot, pt_v, dst_v, mixt, mixf, mixed, ma, ob,
-    qbd, gbd, dko, dvo, p0, p1, fg, wpart, wsa, wra, ws2a, wr2a, wg3a, wg4a,
+    q_v, ks, vs, kst, vst, w_v, cot, scores, pt_v, dst_v, mixt, mixf, mixed, ma, ob,
+    qbd, gbd, inv, base, p0, p1, fg, wpart, wsa, wra, ws2a, wr2a, wg3a, wg4a,
     wsb, wrb, ws2b, wr2b, wg3b, wg4b,
     u0, u1, u2, ru0, ru1, ru2, n3f, h0, h1, h2, rh0, rh1, rh2, fk, fv,
     e0, e1, e2, e3, e4, e5, re0, re1, re2, re3, re4, re5, d3s, rd3,
@@ -82,7 +86,7 @@
     i = pos & 7
     g = pos >> 3
 
-    in_cot = [pltpu.make_async_copy(c_hbm.at[c], cot.at[h, c], in_sem.at[c]) for c in range(4)]
+    in_cot = [pltpu.make_async_copy(c_hbm.at[c], cot.at[block(c), block(h)], in_sem.at[c]) for c in range(4)]
     in_k = [pltpu.make_async_copy(k_hbm.at[t], ks.at[t, pl.ds(0, TILE)], in_sem.at[4 + t]) for t in range(4)]
     in_v = [pltpu.make_async_copy(v_hbm.at[t], vs.at[t, pl.ds(0, TILE)], in_sem.at[8 + t]) for t in range(4)]
     in_q = pltpu.make_async_copy(q_hbm, q_v, in_sem.at[12])
@@ -104,17 +108,21 @@
             device_id=(to_pos, to_head), device_id_type=MESH,
         )
 
+    def ag_copy(way, shard, k, c, to_head):
+        part = cot.at[block(c), block(shard)]
+        return remote(part, part, ag_send.at[way, k, c], ag_recv.at[way, k, c], pos, to_head)
+
     def ag_right(k, c):
-        return remote(cot.at[h - k, c], cot.at[h - k, c], ag_send.at[0, k, c], ag_recv.at[0, k, c], pos, h + 1)
+        return ag_copy(0, h - k, k, c, h + 1)
 
     def ag_left(k, c):
-        return remote(cot.at[h + k, c], cot.at[h + k, c], ag_send.at[1, k, c], ag_recv.at[1, k, c], pos, h - 1)
+        return ag_copy(1, h + k, k, c, h - 1)
 
     def ag_wait_right(k, c):
-        remote(cot.at[h - k, c], cot.at[h - k, c], ag_send.at[0, k - 1, c], ag_recv.at[0, k - 1, c], pos, h).wait_recv()
+        ag_copy(0, h - k, k - 1, c, h).wait_recv()
 
     def ag_wait_left(k, c):
-        remote(cot.at[h + k, c], cot.at[h + k, c], ag_send.at[1, k - 1, c], ag_recv.at[1, k - 1, c], pos, h).wait_recv()
+        ag_copy(1, h + k, k - 1, c, h).wait_recv()
 
     def ag_forward(k, c):
         @pl.when(h - k >= 0)
@@ -257,7 +265,7 @@
 
     def send_mixed(t):
         return remote(
-            mixed.at[t], ma.at[t & 1, h], ma_send.at[t], ma_recv.at[t & 1, h], pos, 1 + (t >> 1)
+            mixed.at[t], ma.at[t & 1, :, block(h)], ma_send.at[t], ma_recv.at[t & 1, h], pos, 1 + (t >> 1)
         )
 
     middle = jnp.logical_and(h > 0, h < 3)
@@ -265,16 +273,40 @@
     def forward(step, carry):
         t = (step + 2 * (1 - (h >> 1))) & 3
         q_tile = q_v[t] * jnp.asarray(0.125, BF)
+
+        def scores_of(hd):
+            q_head = q_tile * head_masks[hd]
+            peak = None
+            for lo in (0, 384):
+                part = mm_nt(ks[t, lo:lo + 384, :], q_head)
+                scores[hd % 2, lo:lo + 384, :] = part
+                part = jnp.max(part.reshape(48, 8, 256), axis=0)
+                peak = part if peak is None else jnp.maximum(peak, part)
+            return jnp.max(peak, axis=0, keepdims=True)
+
+        def weights_of(hd, peak):
+            total = None
+            for lo in range(0, 768, 128):
+                part = jnp.exp(scores[hd % 2, lo:lo + 128, :] - peak)
+                pt_v[t, lo:lo + 128, hd * 256:(hd + 1) * 256] = part.astype(BF)
+                part = jnp.sum(part.reshape(16, 8, 256), axis=0)
+                total = part if total is None else total + part
+            inv[t, hd:hd + 1, :] = 1.0 / jnp.sum(total, axis=0, keepdims=True)
+
+        def mix_of(hd):
+            at = slice(hd * 64, (hd + 1) * 64)
+            mixf[t, at, :] = mm(vst[t, at, :], pt_v[t, :, hd * 256:(hd + 1) * 256]) * inv[t, hd:hd + 1, :]
+
+        peak = scores_of(0)
         for hd in range(4):
-            scores = mm_nt(ks[t], q_tile * head_masks[hd])
-            peak = jnp.max(scores, axis=0, keepdims=True)
-            weights = jnp.exp(scores - peak)
-            total = jnp.sum(weights, axis=0, keepdims=True)
-            probs = (weights * (1.0 / total)).astype(BF)
-            pt_v[t, :, hd * 256:(hd + 1) * 256] = probs
-            mixf[t, hd * 64:(hd + 1) * 64, :] = mm(vst[t, hd * 64:(hd + 1) * 64, :], probs)
+            following = scores_of(hd + 1) if hd < 3 else None
+            weights_of(hd, peak)
+            peak = following
+            if hd > 0:
+                mix_of(hd - 1)
+        mix_of(3)
         whole = mixf[t]
-        mixt[t] = whole.astype(BF)
+        mixt[:, block(t)] = whole.astype(BF)
         mixed[t] = whole.T.astype(BF)
 
         owner = 1 + (t >> 1)
@@ -285,7 +317,7 @@
 
         @pl.when(h == owner)
         def _():
-            ma[t & 1, h] = mixed[t]
+            ma[t & 1, :, block(h)] = mixed[t]
 
         ag_forward(2, step)
         return carry
@@ -304,12 +336,10 @@
 
         def begin(self):
             for j, s in enumerate(self.order):
-                block = mm(mixt[0], cot[s, 0])
-                for t in range(1, 4):
-                    block = block + mm(mixt[t], cot[s, t])
-                wpart[self.first + j] = block
+                part = mm(mixt[...], cot[:, block(s)])
+                wpart[self.first + j] = part
                 for r in range(8):
-                    self.ws[r, :, j * W:(j + 1) * W] = block[r * 32:(r + 1) * 32].astype(BF)
+                    self.ws[r, :, j * W:(j + 1) * W] = part[r * 32:(r + 1) * 32].astype(BF)
             for copy in self.low():
                 copy.start()
 
@@ -405,12 +435,10 @@
             for s in range(4):
                 @pl.when(h != s)
                 def _():
-                    remote(ma.at[tile, s], ma.at[tile, s], ma_send.at[0], ma_recv.at[tile, s], pos, h).wait_recv()
+                    part = ma.at[tile, :, block(s)]
+                    remote(part, part, ma_send.at[0], ma_recv.at[tile, s], pos, h).wait_recv()
             for c in range(4):
-                block = mm(ma[tile, 0], w_v[0:W, c * W:(c + 1) * W])
-                for s in range(1, 4):
-                    block = block + mm(ma[tile, s], w_v[s * W:(s + 1) * W, c * W:(c + 1) * W])
-                ob[tile, c] = block.astype(BF)
+                ob[tile, c] = mm(ma[tile], w_v[:, c * W:(c + 1) * W]).astype(BF)
 
                 @pl.when(h != c)
                 def _():
@@ -420,7 +448,6 @@
                 def _():
                     outr[2 * (h - 1) + tile] = ob[tile, c]
 
-    own_rows = pl.ds(pl.multiple_of(h * W, W), W)
     fg[...] = jnp.zeros_like(fg)
 
     def backward(t, carry):
@@ -432,9 +459,10 @@
         def _():
             ag_wait_left(3, t)
 
-        gmt = mm_nt(w_v[own_rows, 0:W], cot[0, t])
-        for s in range(1, 4):
-            gmt = gmt + mm_nt(w_v[own_rows, s * W:(s + 1) * W], cot[s, t])
+        gmt = mm_nt(w_v[block(h), :], cot[block(t), :])
+        gmt = jnp.concatenate(
+            [gmt[hd * 64:(hd + 1) * 64] * inv[t, hd:hd + 1, :] for hd in range(4)], axis=0
+        )
         @pl.when(t == 2)
         def _():
             part_a.to_high()
@@ -446,26 +474,30 @@
         gm = gmt.T.astype(BF)
         gmt = gmt.astype(BF).astype(F32)
         q_tile = q_v[t] * jnp.asarray(0.125, BF)
+        for hd in range(4):
+            part = slice(hd * 256, (hd + 1) * 256)
+            gbd[part, :] = gm * head_masks[hd]
+            qbd[part, :] = q_tile * head_masks[hd]
+        for hd in range(4):
+            at = slice(hd * 64, (hd + 1) * 64)
+            part = slice(hd * 256, (hd + 1) * 256)
+            centre = jnp.sum(gmt[at] * mixf[t, at, :], axis=0, keepdims=True)
+            for lo in range(0, 768, 256):
+                rows = slice(lo, lo + 256)
+                grad_probs = mm_nt(vs[t, rows, :], gbd[part, :])
+                dst_v[rows, part] = (pt_v[t, rows, part].astype(F32) * (grad_probs - centre)).astype(BF)
         dqt = []
         for hd in range(4):
             at = slice(hd * 64, (hd + 1) * 64)
-            block = slice(hd * 256, (hd + 1) * 256)
-            gm_head = gm * head_masks[hd]
-            gbd[block, :] = gm_head
-            qbd[block, :] = q_tile * head_masks[hd]
-            centre = jnp.sum(gmt[at] * mixf[t, at, :], axis=0, keepdims=True)
-            grad_probs = mm_nt(vs[t], gm_head)
-            dscore = (pt_v[t, :, block].astype(F32) * (grad_probs - centre)).astype(BF)
-            dst_v[:, block] = dscore
-            dqt.append(mm(kst[t, at, :], dscore))
+            dqt.append(mm(kst[t, at, :], dst_v[:, hd * 256:(hd + 1) * 256]))
         gq_v[t] = (jnp.concatenate(dqt, axis=0) * 0.125).T.astype(BF)
-        dk = mm(dst_v[...], qbd[...])
-        dv = mm(pt_v[t], gbd[...])
-        dko[t] = dk[0:256]
-        dvo[t] = dv[0:256]
+        dk = mm(dst_v[0:384, :], qbd[...])
+        dv = mm(pt_v[t, 0:384, :], gbd[...])
+        base[t] = lanes(dk[0:256], dv[0:256])
         p0[t] = lanes(dk[256:320], dv[256:320])
         p1[t] = lanes(dk[320:384], dv[320:384])
-        fg[...] += lanes(dk[384:768], dv[384:768])
+        fg[:, :W] += mm(dst_v[384:768, :], qbd[...])
+        fg[:, W:] += mm(pt_v[t, 384:768, :], gbd[...])
         return carry
 
     lax.fori_loop(0, 4, backward, 0)
@@ -505,23 +537,37 @@
         dl[-1].start()
 
     part_a.to_back_x()
+    part_b.to_high()
 
     @pl.when(middle)
     def _():
         project()
 
-    part_b.to_high()
+    def f32_kv(x):
+        return unstack_kv(x.astype(F32))
+
+    def total_of(buffer, count):
+        total = f32_kv(buffer[0])
+        for k in range(1, count):
+            total = total + f32_kv(buffer[k])
+        return total
+
+    for copy in dl:
+        copy.wait_recv()
+    top_grad = f32_kv(re0[...]) + spread(total_of(re1, 2), 1) + spread(total_of(re2, 4), 2)
+    for n in range(2):
+        first = 2 * (1 - n)
+        down_1 = p1[first] + p1[first + 1] + spread(top_grad[n * 32:(n + 1) * 32], 1)
+        for r in range(2):
+            t = 2 * n + r
+            down_0 = p0[t ^ 1] + spread(down_1[r * 32:(r + 1) * 32], 1)
+            base[t] += repeat_rows(down_0, 2) * 0.5
     part_a.to_back_low()
 
     for copy in dh:
         copy.wait_recv()
 
-    def f32_kv(x):
-        return unstack_kv(x.astype(F32))
-
-    quarter = f32_kv(re5[0]) + f32_kv(re5[1]) + f32_kv(re5[2]) + f32_kv(re5[3])
-    half = f32_kv(re4[0]) + f32_kv(re4[1]) + spread2(quarter)
-    group_grad = f32_kv(re3[...]) + spread2(half)
+    group_grad = f32_kv(re3[...]) + spread(total_of(re4, 2), 1) + spread(total_of(re5, 4), 2)
     for r in range(8):
         d3s[r] = stack_kv(group_grad[r * 8:(r + 1) * 8]).astype(BF)
     d3 = []
@@ -531,27 +577,18 @@
 
     part_b.to_back_x()
 
-    for copy in dl:
-        copy.wait_recv()
     for copy in d3:
         copy.wait_recv()
     eighth = f32_kv(d3s[i])
     for m in range(1, 8):
         eighth = eighth + f32_kv(rd3[m])
-    quarter = f32_kv(re2[0]) + f32_kv(re2[1]) + f32_kv(re2[2]) + f32_kv(re2[3]) + spread2(eighth)
-    half = f32_kv(re1[0]) + f32_kv(re1[1]) + spread2(quarter)
-    top_grad = f32_kv(re0[...]) + spread2(half)
-    spread_top = spread2(top_grad)
-    for n in range(2):
-        first = 2 * (1 - n)
-        down_1 = p1[first] + p1[first + 1] + spread_top[n * 64:(n + 1) * 64]
-        spread_1 = spread2(down_1)
-        for r in range(2):
-            t = 2 * n + r
-            down_0 = p0[t ^ 1] + spread_1[r * 64:(r + 1) * 64]
-            back = repeat_rows(down_0, 2) * 0.5
-            gk_v[t] = (dko[t] + back[:, :W]).astype(BF)
-            gv_v[t] = (dvo[t] + back[:, W:]).astype(BF)
+    eighth = eighth * (0.25 * ROOT_HALF ** 3)
+    for t in range(4):
+        for half in range(2):
+            rows = slice(half * 128, (half + 1) * 128)
+            whole = base[t, rows, :] + eighth[2 * t + half:2 * t + half + 1, :]
+            gk_v[t, rows, :] = whole[:, :W].astype(BF)
+            gv_v[t, rows, :] = whole[:, W:].astype(BF)
     part_b.to_back_low()
     part_a.finish()
     for t in range(4):
@@ -616,10 +653,10 @@
     dma = pltpu.SemaphoreType.DMA
     scratch = [
         v(4, 256, 256), v(4, 768, 256), v(4, 768, 256), v(4, 256, 768), v(4, 256, 768),
-        v(1024, 1024), v(4, 4, 256, 256), v(4, 768, 1024), v(768, 1024),
-        v(4, 256, 256), f(4, 256, 256), v(4, 256, 256), v(2, 4, 256, 256),
+        v(1024, 1024), v(1024, 1024), f(2, 768, 256), v(4, 768, 1024), v(768, 1024),
+        v(256, 1024), f(4, 256, 256), v(4, 256, 256), v(2, 256, 1024),
         v(2, 4, 256, 256),
-        v(1024, 256), v(1024, 256), f(4, 256, 256), f(4, 256, 256),
+        v(1024, 256), v(1024, 256), f(4, 8, 256), f(4, 256, 512),
         f(4, 64, 512), f(4, 64, 512), f(384, 512), f(4, 256, 256),
         v(8, 32, 768), v(8, 32, 768), v(4, 16, 384), v(8, 16, 384), v(4, 16, 384), v(8, 4, 16, 384),
         v(8, 32, 256), v(8, 32, 256), v(4, 16, 128), v(8, 16, 128), v(4, 16, 128), v(8, 4, 16, 128),

time: 84.6 us -> 78.1 us (0.923)
  Pallas kernels: 83.9 us -> 77.4 us
    pallas_call x1, Pallas kernels: 82.2 us -> 75.7 us  [local(): pl.pallas_call(kernel, out_shape=out_shape, in_specs=[pl.BlockSpec(memory...]
where the time goes in v3:
time: 78.1 us; the launch traced here: 78 us
  Pallas kernels  77.4 us (99%)
    pallas_call x1, Pallas kernels, local(): pl.pallas_call(kernel, out_shape=out_shape, in_specs=[pl.BlockSpec(memory...  75.7 us
    pallas_call x1, Pallas kernels, hand_over(): pl.pallas_call(copy_kernel, out_shape=[jax.ShapeDtypeStruct(a.shape, a.dt...  1.71 us

profile of v3, /device:TPU:33, one launch (start us, length us, event | category | flops | bytes accessed | tf_op | source)
XLA Modules:
  0.0 78.0 jit_solution(10701029905225499277)
XLA Ops:
  0.6 75.7 %shard_map.92 = (bf16[4,256,256]{2,1,0:T(8,128)(2,1)S(1)}, bf16[4,256,256]{2,1,0:T(8,128)(2,1)S(1)}, bf16[4,256,256]{2,1,0:T(8,128)(2,1)S(1)}, bf16[4,256,256]{2,1,0:T(8,128)(2,1)S(1)}, f32[256,1024]{1,0:T(8,128)S(1)}) custom-call(bf16[4,256,256]{2,1,0:T(8,128)(2,1)} %bitcast.8, bf16[4,256,256]{2,1,0:T(8,128)(2,1)} %bitcast.9, ...), custom_call_target="tpu_custom_call" | custom-call | tf_op jit(solution)/shard_map/pallas_call | solution.py:674
  76.3 1.7 %shard_map.93 = (bf16[4,256,256]{2,1,0:T(8,128)(2,1)}, bf16[4,256,256]{2,1,0:T(8,128)(2,1)}, bf16[4,256,256]{2,1,0:T(8,128)(2,1)}, bf16[4,256,256]{2,1,0:T(8,128)(2,1)}, f32[256,1024]{1,0:T(8,128)}) custom-call(bf16[4,256,256]{2,1,0:T(8,128)(2,1)S(1)} %get-tuple-element.15.refs_0_, bf16[4,256,256]{2,1,0:T(8,128)(2,1)S(1)} %get-tuple-element.16.refs_1_, ...), custom_call_target="tpu_custom_call" | custom-call | tf_op jit(solution)/shard_map/pallas_call | solution.py:635

commit v4 on v3

--- a/solution.py
+++ b/solution.py
@@ -166,6 +166,15 @@
         copy.wait()
     pl.semaphore_wait(barrier, 17)
 
+    for c in range(4):
+        @pl.when(h < 3)
+        def _():
+            ag_right(0, c).start()
+
+        @pl.when(h > 0)
+        def _():
+            ag_left(0, c).start()
+
     def low_pair(m, s0, r0, s1, r1, s2, r2):
         if m == 1:
             return s0, r0
@@ -178,15 +187,6 @@
         src, dst = low_pair(m, u0, ru0, u1, ru1, u2, ru2)
         up.append(remote(src, dst, up_send.at[m - 1], up_recv.at[m - 1], pos ^ m, h))
         up[-1].start()
-
-    for c in range(4):
-        @pl.when(h < 3)
-        def _():
-            ag_right(0, c).start()
-
-        @pl.when(h > 0)
-        def _():
-            ag_left(0, c).start()
 
     for t in range(4):
         other = leaf[t ^ 1]
@@ -319,7 +319,10 @@
         def _():
             ma[t & 1, :, block(h)] = mixed[t]
 
-        ag_forward(2, step)
+        @pl.when(jnp.logical_and(middle, step > 0))
+        def _():
+            ag_forward(2, step - 1)
+
         return carry
 
     lax.fori_loop(0, 4, forward, 0)
@@ -420,15 +423,72 @@
             lax.fori_loop(0, 8, put, 0)
 
         def wait_sends(self):
-            for copy in self.low() + self.high() + self.back_x() + self.back_low():
+            for copy in self.low() + self.high() + self.back_x():
                 copy.wait_send()
 
+        def wait_back(self):
+            for copy in self.back_low():
+                copy.wait_send()
+
+    class Last(Reduction):
+        def high(self):
+            return [
+                remote(self.ws2, self.wr2.at[g], w2_send.at[self.part, m - 1], w2_recv.at[self.part, m - 1], pos ^ (8 * m), h)
+                for m in range(1, 8)
+            ]
+
+        def to_high(self):
+            for copy in self.low():
+                copy.wait_recv()
+            total = wpart[self.first, pl.ds(pl.multiple_of(i * 32, 32), 32), :]
+            for m in range(1, 8):
+                total = total + self.wr[m].astype(F32)
+            self.ws2[...] = total.astype(BF)
+            for copy in self.high():
+                copy.start()
+            self.wr2[g] = self.ws2[...]
+
+        def to_back_low(self):
+            for m in range(1, 8):
+                remote(self.ws2, self.wr2.at[g ^ m], w2_send.at[self.part, m - 1], w2_recv.at[self.part, m - 1], pos, h).wait_recv()
+            total = self.wr2[0].astype(F32)
+            for r in range(1, 8):
+                total = total + self.wr2[r].astype(F32)
+            self.wg3[...] = total.astype(BF)
+            for copy in self.back_low():
+                copy.start()
+            self.wg4[0] = self.wg3[...]
+
+        def finish(self):
+            for copy in self.back_low():
+                copy.wait_recv()
+            for m in range(8):
+                wgo[pl.ds(pl.multiple_of((i ^ m) * 32, 32), 32), block(self.order[0])] = self.wg4[m].astype(F32)
+
+        def wait_sends(self):
+            for copy in self.low() + self.high():
+                copy.wait_send()
+
     part_a = Reduction(order_a, 0, (wsa, wra, ws2a, wr2a, wg3a, wg4a))
-    part_b = Reduction(order_b, 1, (wsb, wrb, ws2b, wr2b, wg3b, wg4b))
+    part_b = Last(order_b, 1, (wsb, wrb, ws2b, wr2b, wg3b, wg4b))
+
+    @pl.when(jnp.logical_not(middle))
+    def _():
+        for c in range(4):
+            ag_forward(2, c)
+
     part_a.begin()
+
+    @pl.when(middle)
+    def _():
+        ag_forward(2, 3)
 
     def send_output(tile, c):
         return remote(ob.at[tile, c], outr.at[2 * (h - 1) + tile], ob_send.at[tile, c], ob_recv.at[2 * (h - 1) + tile], pos, c)
+
+    def send_tile(tile):
+        for m in (2, 3, 1):
+            send_output(tile, h ^ m).start()
 
     def project():
         for tile in range(2):
@@ -437,16 +497,12 @@
                 def _():
                     part = ma.at[tile, :, block(s)]
                     remote(part, part, ma_send.at[0], ma_recv.at[tile, s], pos, h).wait_recv()
+        for tile in range(2):
             for c in range(4):
                 ob[tile, c] = mm(ma[tile], w_v[:, c * W:(c + 1) * W]).astype(BF)
-
-                @pl.when(h != c)
-                def _():
-                    send_output(tile, c).start()
-
-                @pl.when(h == c)
-                def _():
-                    outr[2 * (h - 1) + tile] = ob[tile, c]
+        for tile in range(2):
+            outr[2 * (h - 1) + tile] = ob[tile, h]
+        send_tile(0)
 
     fg[...] = jnp.zeros_like(fg)
 
@@ -463,11 +519,7 @@
         gmt = jnp.concatenate(
             [gmt[hd * 64:(hd + 1) * 64] * inv[t, hd:hd + 1, :] for hd in range(4)], axis=0
         )
-        @pl.when(t == 2)
-        def _():
-            part_a.to_high()
-
-        @pl.when(t == 3)
+        @pl.when(t == 3 * (1 - (((h + 1) >> 1) & 1)))
         def _():
             part_b.begin()
 
@@ -498,6 +550,15 @@
         p1[t] = lanes(dk[320:384], dv[320:384])
         fg[:, :W] += mm(dst_v[384:768, :], qbd[...])
         fg[:, W:] += mm(pt_v[t, 384:768, :], gbd[...])
+
+        @pl.when(t == 2)
+        def _():
+            part_a.to_high()
+
+            @pl.when(middle)
+            def _():
+                part_b.to_high()
+
         return carry
 
     lax.fori_loop(0, 4, backward, 0)
@@ -527,6 +588,15 @@
         src, dst = down_pair(m, g, e3, re3, e4, re4, e5, re5)
         dh.append(remote(src, dst, dh_send.at[m - 1], dh_recv.at[m - 1], pos ^ (8 * m), h))
         dh[-1].start()
+    @pl.when(middle)
+    def _():
+        project()
+
+    @pl.when(jnp.logical_not(middle))
+    def _():
+        part_b.to_high()
+
+    part_a.to_back_x()
     e0[...] = stack_kv(level(0)).astype(BF)
     cut(e1, 1, 2)
     cut(e2, 2, 4)
@@ -536,12 +606,8 @@
         dl.append(remote(src, dst, dl_send.at[m - 1], dl_recv.at[m - 1], pos ^ m, h))
         dl[-1].start()
 
-    part_a.to_back_x()
-    part_b.to_high()
-
-    @pl.when(middle)
-    def _():
-        project()
+
+    part_a.to_back_low()
 
     def f32_kv(x):
         return unstack_kv(x.astype(F32))
@@ -551,6 +617,39 @@
         for k in range(1, count):
             total = total + f32_kv(buffer[k])
         return total
+
+    for copy in up + uh:
+        copy.wait_send()
+    for t in range(4):
+        @pl.when(h != 1 + (t >> 1))
+        def _():
+            send_mixed(t).wait_send()
+    for k in range(3):
+        for c in range(4):
+            @pl.when(jnp.logical_and(h - k >= 0, h < 3))
+            def _():
+                ag_right(k, c).wait_send()
+
+            @pl.when(jnp.logical_and(h + k <= 3, h > 0))
+            def _():
+                ag_left(k, c).wait_send()
+
+    for copy in dh:
+        copy.wait_recv()
+
+    group_grad = f32_kv(re3[...]) + spread(total_of(re4, 2), 1) + spread(total_of(re5, 4), 2)
+    for r in range(8):
+        d3s[r] = stack_kv(group_grad[r * 8:(r + 1) * 8]).astype(BF)
+    d3 = []
+    for m in range(1, 8):
+        d3.append(remote(d3s.at[i ^ m], rd3.at[m], d3_send.at[m - 1], d3_recv.at[m - 1], pos ^ m, h))
+        d3[-1].start()
+
+    part_b.to_back_low()
+
+    @pl.when(middle)
+    def _():
+        send_tile(1)
 
     for copy in dl:
         copy.wait_recv()
@@ -562,21 +661,11 @@
             t = 2 * n + r
             down_0 = p0[t ^ 1] + spread(down_1[r * 32:(r + 1) * 32], 1)
             base[t] += repeat_rows(down_0, 2) * 0.5
-    part_a.to_back_low()
-
-    for copy in dh:
-        copy.wait_recv()
-
-    group_grad = f32_kv(re3[...]) + spread(total_of(re4, 2), 1) + spread(total_of(re5, 4), 2)
-    for r in range(8):
-        d3s[r] = stack_kv(group_grad[r * 8:(r + 1) * 8]).astype(BF)
-    d3 = []
-    for m in range(1, 8):
-        d3.append(remote(d3s.at[i ^ m], rd3.at[m], d3_send.at[m - 1], d3_recv.at[m - 1], pos ^ m, h))
-        d3[-1].start()
-
-    part_b.to_back_x()
-
+
+    for copy in dl + dh:
+        copy.wait_send()
+    part_a.wait_sends()
+    part_b.wait_sends()
     for copy in d3:
         copy.wait_recv()
     eighth = f32_kv(d3s[i])
@@ -589,7 +678,6 @@
             whole = base[t, rows, :] + eighth[2 * t + half:2 * t + half + 1, :]
             gk_v[t, rows, :] = whole[:, :W].astype(BF)
             gv_v[t, rows, :] = whole[:, W:].astype(BF)
-    part_b.to_back_low()
     part_a.finish()
     for t in range(4):
         @pl.when(h != 1 + (t >> 1))
@@ -597,28 +685,15 @@
             remote(outr.at[t], outr.at[t], ob_send.at[0, 0], ob_recv.at[t], pos, h).wait_recv()
     part_b.finish()
 
-    for copy in up + uh + dl + dh + d3:
+    for copy in d3:
         copy.wait_send()
-    part_a.wait_sends()
-    part_b.wait_sends()
-    for t in range(4):
-        @pl.when(h != 1 + (t >> 1))
-        def _():
-            send_mixed(t).wait_send()
+    part_a.wait_back()
+    part_b.wait_back()
     for tile in range(2):
         for c in range(4):
             @pl.when(jnp.logical_and(middle, h != c))
             def _():
                 send_output(tile, c).wait_send()
-    for k in range(3):
-        for c in range(4):
-            @pl.when(jnp.logical_and(h - k >= 0, h < 3))
-            def _():
-                ag_right(k, c).wait_send()
-
-            @pl.when(jnp.logical_and(h + k <= 3, h > 0))
-            def _():
-                ag_left(k, c).wait_send()
 
 
 def hand_over(*arrays):
@@ -626,7 +701,12 @@
 
     def copy_kernel(*refs):
         sems = refs[2 * n]
-        copies = [pltpu.make_async_copy(refs[k], refs[n + k], sems.at[k]) for k in range(n)]
+        copies = []
+        for k in range(n):
+            size = arrays[k].shape[0] // 4
+            for part in range(4):
+                cut = pl.ds(part * size, size)
+                copies.append(pltpu.make_async_copy(refs[k].at[cut], refs[n + k].at[cut], sems.at[k, part]))
         for copy in copies:
             copy.start()
         for copy in copies:
@@ -637,7 +717,7 @@
         out_shape=[jax.ShapeDtypeStruct(a.shape, a.dtype) for a in arrays],
         in_specs=[pl.BlockSpec(memory_space=pltpu.VMEM)] * n,
         out_specs=[pl.BlockSpec(memory_space=pltpu.HBM)] * n,
-        scratch_shapes=[pltpu.SemaphoreType.DMA((n,))],
+        scratch_shapes=[pltpu.SemaphoreType.DMA((n, 4))],
     )(*[pltpu.with_memory_space_constraint(a, pltpu.VMEM) for a in arrays])
 
 
@@ -659,7 +739,7 @@
         v(1024, 256), v(1024, 256), f(4, 8, 256), f(4, 256, 512),
         f(4, 64, 512), f(4, 64, 512), f(384, 512), f(4, 256, 256),
         v(8, 32, 768), v(8, 32, 768), v(4, 16, 384), v(8, 16, 384), v(4, 16, 384), v(8, 4, 16, 384),
-        v(8, 32, 256), v(8, 32, 256), v(4, 16, 128), v(8, 16, 128), v(4, 16, 128), v(8, 4, 16, 128),
+        v(8, 32, 256), v(8, 32, 256), v(32, 256), v(8, 32, 256), v(32, 256), v(8, 32, 256),
         v(144, 256), v(80, 256), v(48, 256), v(144, 256), v(2, 80, 256), v(4, 48, 256),
         f(64, 512), v(128, 256), v(64, 256), v(32, 256),
         v(128, 256), v(2, 64, 256), v(4, 32, 256), v(384, 256), v(384, 256),

time: 78.1 us -> 74.9 us (0.959)
  the two profiles are of different devices: /device:TPU:33 before, /device:TPU:1 now
where the time goes in v4:
time: 74.9 us; the launch traced here: 74.8 us
  Pallas kernels  74.2 us (99%)
    pallas_call x1, Pallas kernels, local(): pl.pallas_call(kernel, out_shape=out_shape, in_specs=[pl.BlockSpec(memory...  72.4 us
    pallas_call x1, Pallas kernels, hand_over(): pl.pallas_call(copy_kernel, out_shape=[jax.ShapeDtypeStruct(a.shape, a.dt...  1.83 us

profile of v4, /device:TPU:1, one launch (start us, length us, event | category | flops | bytes accessed | tf_op | source)
XLA Modules:
  0.0 74.8 jit_solution(4426311933025911568)
XLA Ops:
  0.6 72.4 %shard_map.92 = (bf16[4,256,256]{2,1,0:T(8,128)(2,1)S(1)}, bf16[4,256,256]{2,1,0:T(8,128)(2,1)S(1)}, bf16[4,256,256]{2,1,0:T(8,128)(2,1)S(1)}, bf16[4,256,256]{2,1,0:T(8,128)(2,1)S(1)}, f32[256,1024]{1,0:T(8,128)S(1)}) custom-call(bf16[4,256,256]{2,1,0:T(8,128)(2,1)} %bitcast.8, bf16[4,256,256]{2,1,0:T(8,128)(2,1)} %bitcast.9, ...), custom_call_target="tpu_custom_call" | custom-call | tf_op jit(solution)/shard_map/pallas_call | solution.py:754
  73.0 1.8 %shard_map.93 = (bf16[4,256,256]{2,1,0:T(8,128)(2,1)}, bf16[4,256,256]{2,1,0:T(8,128)(2,1)}, bf16[4,256,256]{2,1,0:T(8,128)(2,1)}, bf16[4,256,256]{2,1,0:T(8,128)(2,1)}, f32[256,1024]{1,0:T(8,128)}) custom-call(bf16[4,256,256]{2,1,0:T(8,128)(2,1)S(1)} %get-tuple-element.15.refs_0_, bf16[4,256,256]{2,1,0:T(8,128)(2,1)S(1)} %get-tuple-element.16.refs_1_, ...), custom_call_target="tpu_custom_call" | custom-call | tf_op jit(solution)/shard_map/pallas_call | solution.py:715

commit v5 on v4

--- a/solution.py
+++ b/solution.py
@@ -53,6 +53,11 @@
 
 def block(k):
     return pl.ds(pl.multiple_of(k * W, W), W)
+
+
+def start_far_first(copies):
+    for m in (4, 5, 6, 7, 2, 3, 1):
+        copies[m - 1].start()
 
 
 def lanes(a, b):
@@ -166,15 +171,6 @@
         copy.wait()
     pl.semaphore_wait(barrier, 17)
 
-    for c in range(4):
-        @pl.when(h < 3)
-        def _():
-            ag_right(0, c).start()
-
-        @pl.when(h > 0)
-        def _():
-            ag_left(0, c).start()
-
     def low_pair(m, s0, r0, s1, r1, s2, r2):
         if m == 1:
             return s0, r0
@@ -186,7 +182,16 @@
     for m in range(1, 8):
         src, dst = low_pair(m, u0, ru0, u1, ru1, u2, ru2)
         up.append(remote(src, dst, up_send.at[m - 1], up_recv.at[m - 1], pos ^ m, h))
-        up[-1].start()
+    start_far_first(up)
+    for c in range(4):
+        @pl.when(h < 3)
+        def _():
+            ag_right(0, c).start()
+
+        @pl.when(h > 0)
+        def _():
+            ag_left(0, c).start()
+
 
     for t in range(4):
         other = leaf[t ^ 1]
@@ -234,7 +239,7 @@
     for m in range(1, 8):
         src, dst = low_pair(m, h0, rh0, h1, rh1, h2, rh2)
         uh.append(remote(src, dst, uh_send.at[m - 1], uh_recv.at[m - 1], pos ^ (8 * m), h))
-        uh[-1].start()
+    start_far_first(uh)
 
     for c in range(4):
         ag_forward(1, c)
@@ -343,8 +348,7 @@
                 wpart[self.first + j] = part
                 for r in range(8):
                     self.ws[r, :, j * W:(j + 1) * W] = part[r * 32:(r + 1) * 32].astype(BF)
-            for copy in self.low():
-                copy.start()
+            start_far_first(self.low())
 
         def low(self):
             return [
@@ -383,8 +387,7 @@
             for r in range(4):
                 piece = total[r * 8:(r + 1) * 8]
                 self.ws2[r] = jnp.concatenate([piece[:, :half], piece[:, half:]], axis=0).astype(BF)
-            for copy in self.high():
-                copy.start()
+            start_far_first(self.high())
             self.wr2[g] = self.ws2[g & 3]
 
         def to_back_x(self):
@@ -401,8 +404,7 @@
             for m in range(1, 4):
                 slot = self.wg3.at[(g ^ m) & 3]
                 remote(slot, slot, w3_send.at[self.part, m - 1], w3_recv.at[self.part, m - 1], pos, h).wait_recv()
-            for copy in self.back_low():
-                copy.start()
+            start_far_first(self.back_low())
             self.wg4[0] = self.wg3[...]
 
         def finish(self):
@@ -444,8 +446,7 @@
             for m in range(1, 8):
                 total = total + self.wr[m].astype(F32)
             self.ws2[...] = total.astype(BF)
-            for copy in self.high():
-                copy.start()
+            start_far_first(self.high())
             self.wr2[g] = self.ws2[...]
 
         def to_back_low(self):
@@ -455,8 +456,7 @@
             for r in range(1, 8):
                 total = total + self.wr2[r].astype(F32)
             self.wg3[...] = total.astype(BF)
-            for copy in self.back_low():
-                copy.start()
+            start_far_first(self.back_low())
             self.wg4[0] = self.wg3[...]
 
         def finish(self):
@@ -587,7 +587,7 @@
     for m in range(1, 8):
         src, dst = down_pair(m, g, e3, re3, e4, re4, e5, re5)
         dh.append(remote(src, dst, dh_send.at[m - 1], dh_recv.at[m - 1], pos ^ (8 * m), h))
-        dh[-1].start()
+    start_far_first(dh)
     @pl.when(middle)
     def _():
         project()
@@ -604,7 +604,7 @@
     for m in range(1, 8):
         src, dst = down_pair(m, i, e0, re0, e1, re1, e2, re2)
         dl.append(remote(src, dst, dl_send.at[m - 1], dl_recv.at[m - 1], pos ^ m, h))
-        dl[-1].start()
+    start_far_first(dl)
 
 
     part_a.to_back_low()
@@ -643,7 +643,7 @@
     d3 = []
     for m in range(1, 8):
         d3.append(remote(d3s.at[i ^ m], rd3.at[m], d3_send.at[m - 1], d3_recv.at[m - 1], pos ^ m, h))
-        d3[-1].start()
+    start_far_first(d3)
 
     part_b.to_back_low()
 

time: 74.9 us -> 74.6 us (level)
  no operation moved by 1% of the time
where the time goes in v5:
time: 74.6 us; the launch traced here: 74.5 us
  Pallas kernels  73.8 us (99%)
    pallas_call x1, Pallas kernels, local(): pl.pallas_call(kernel, out_shape=out_shape, in_specs=[pl.BlockSpec(memory...  72 us
    pallas_call x1, Pallas kernels, hand_over(): pl.pallas_call(copy_kernel, out_shape=[jax.ShapeDtypeStruct(a.shape, a.dt...  1.83 us

profile of v5, /device:TPU:1, one launch (start us, length us, event | category | flops | bytes accessed | tf_op | source)
XLA Modules:
  0.0 74.5 jit_solution(16863199452301986750)
XLA Ops:
  0.6 72.0 %shard_map.92 = (bf16[4,256,256]{2,1,0:T(8,128)(2,1)S(1)}, bf16[4,256,256]{2,1,0:T(8,128)(2,1)S(1)}, bf16[4,256,256]{2,1,0:T(8,128)(2,1)S(1)}, bf16[4,256,256]{2,1,0:T(8,128)(2,1)S(1)}, f32[256,1024]{1,0:T(8,128)S(1)}) custom-call(bf16[4,256,256]{2,1,0:T(8,128)(2,1)} %bitcast.8, bf16[4,256,256]{2,1,0:T(8,128)(2,1)} %bitcast.9, ...), custom_call_target="tpu_custom_call" | custom-call | tf_op jit(solution)/shard_map/pallas_call | solution.py:754
  72.7 1.8 %shard_map.93 = (bf16[4,256,256]{2,1,0:T(8,128)(2,1)}, bf16[4,256,256]{2,1,0:T(8,128)(2,1)}, bf16[4,256,256]{2,1,0:T(8,128)(2,1)}, bf16[4,256,256]{2,1,0:T(8,128)(2,1)}, f32[256,1024]{1,0:T(8,128)}) custom-call(bf16[4,256,256]{2,1,0:T(8,128)(2,1)S(1)} %get-tuple-element.15.refs_0_, bf16[4,256,256]{2,1,0:T(8,128)(2,1)S(1)} %get-tuple-element.16.refs_1_, ...), custom_call_target="tpu_custom_call" | custom-call | tf_op jit(solution)/shard_map/pallas_call | solution.py:715

commit v6 on v5

--- a/solution.py
+++ b/solution.py
@@ -666,6 +666,7 @@
         copy.wait_send()
     part_a.wait_sends()
     part_b.wait_sends()
+    part_a.finish()
     for copy in d3:
         copy.wait_recv()
     eighth = f32_kv(d3s[i])
@@ -678,7 +679,6 @@
             whole = base[t, rows, :] + eighth[2 * t + half:2 * t + half + 1, :]
             gk_v[t, rows, :] = whole[:, :W].astype(BF)
             gv_v[t, rows, :] = whole[:, W:].astype(BF)
-    part_a.finish()
     for t in range(4):
         @pl.when(h != 1 + (t >> 1))
         def _():
@@ -701,12 +701,7 @@
 
     def copy_kernel(*refs):
         sems = refs[2 * n]
-        copies = []
-        for k in range(n):
-            size = arrays[k].shape[0] // 4
-            for part in range(4):
-                cut = pl.ds(part * size, size)
-                copies.append(pltpu.make_async_copy(refs[k].at[cut], refs[n + k].at[cut], sems.at[k, part]))
+        copies = [pltpu.make_async_copy(refs[k], refs[n + k], sems.at[k]) for k in range(n)]
         for copy in copies:
             copy.start()
         for copy in copies:
@@ -717,7 +712,7 @@
         out_shape=[jax.ShapeDtypeStruct(a.shape, a.dtype) for a in arrays],
         in_specs=[pl.BlockSpec(memory_space=pltpu.VMEM)] * n,
         out_specs=[pl.BlockSpec(memory_space=pltpu.HBM)] * n,
-        scratch_shapes=[pltpu.SemaphoreType.DMA((n, 4))],
+        scratch_shapes=[pltpu.SemaphoreType.DMA((n,))],
     )(*[pltpu.with_memory_space_constraint(a, pltpu.VMEM) for a in arrays])
 
 

time: 74.6 us -> 74.4 us (level)
  no operation moved by 1% of the time
where the time goes in v6:
time: 74.4 us
  Pallas kernels  73.7 us (99%)
    pallas_call x1, Pallas kernels, local(): pl.pallas_call(kernel, out_shape=out_shape, in_specs=[pl.BlockSpec(memory...  72 us
    pallas_call x1, Pallas kernels, hand_over(): pl.pallas_call(copy_kernel, out_shape=[jax.ShapeDtypeStruct(a.shape, a.dt...  1.71 us

profile of v6, /device:TPU:1, one launch (start us, length us, event | category | flops | bytes accessed | tf_op | source)
XLA Modules:
  0.0 74.4 jit_solution(5930219292205498672)
XLA Ops:
  0.6 72.0 %shard_map.92 = (bf16[4,256,256]{2,1,0:T(8,128)(2,1)S(1)}, bf16[4,256,256]{2,1,0:T(8,128)(2,1)S(1)}, bf16[4,256,256]{2,1,0:T(8,128)(2,1)S(1)}, bf16[4,256,256]{2,1,0:T(8,128)(2,1)S(1)}, f32[256,1024]{1,0:T(8,128)S(1)}) custom-call(bf16[4,256,256]{2,1,0:T(8,128)(2,1)} %bitcast.8, bf16[4,256,256]{2,1,0:T(8,128)(2,1)} %bitcast.9, ...), custom_call_target="tpu_custom_call" | custom-call | tf_op jit(solution)/shard_map/pallas_call | solution.py:749
  72.7 1.7 %shard_map.93 = (bf16[4,256,256]{2,1,0:T(8,128)(2,1)}, bf16[4,256,256]{2,1,0:T(8,128)(2,1)}, bf16[4,256,256]{2,1,0:T(8,128)(2,1)}, bf16[4,256,256]{2,1,0:T(8,128)(2,1)}, f32[256,1024]{1,0:T(8,128)}) custom-call(bf16[4,256,256]{2,1,0:T(8,128)(2,1)S(1)} %get-tuple-element.15.refs_0_, bf16[4,256,256]{2,1,0:T(8,128)(2,1)S(1)} %get-tuple-element.16.refs_1_, ...), custom_call_target="tpu_custom_call" | custom-call | tf_op jit(solution)/shard_map/pallas_call | solution.py:710
